TPU v7x, 32 devices: a whole 2x2x4 slice. The times are simulated.
32 devices in a mesh: space: 8 (over y, x, core), chaos: 4 (over z).
Axes of the slice: x: 2, y: 2, z: 4, core: 2. Of those that a mesh axis runs over, the one named last changes fastest.
Arguments:
- field: bfloat16 [168, 131072], P('chaos', 'space'), may hold values from -6 to 6
- stiffness: bfloat16 [2048, 4096], P(('space', 'chaos')), may hold values from -0.75 to 0.75
- kl_coef: float32 [9, 2048], P(None, ('space', 'chaos')), may hold values from -3 to 3
- triple_mode: int32 [2688], replicated, may hold values from 0 to 7
- triple_row: int32 [2688], replicated, may hold values from 0 to 167
- triple_col: int32 [2688], replicated, may hold values from 0 to 167
- triple_value: float32 [2688], replicated, may hold values from -3 to 3
- die_elem: int32 [4096], P(('space', 'chaos')), may hold values from 0 to 63
- die_side: int32 [4096], P(('space', 'chaos')), may hold values from 0 to 5
- seg_owner: int32 [4096], P(('space', 'chaos')), may hold values from 0 to 31, as said below
- seg_face: int32 [4096], P(('space', 'chaos')), may hold values from 0 to 63
- die_mortar: bfloat16 [4096, 256], P(('space', 'chaos')), may hold values from -1.5 to 1.5
- int_mortar: bfloat16 [4096, 256], P(('space', 'chaos')), may hold values from -1.5 to 1.5
- bump_coef: bfloat16 [4096, 9], P(('space', 'chaos')), may hold values from -3 to 3
- int_elem: int32 [2048], P(('space', 'chaos')), may hold values from 0 to 63
- int_side: int32 [2048], P(('space', 'chaos')), may hold values from 0 to 5
Outputs:
- response: bfloat16 [168, 131072], P('chaos', 'space')
Inputs may be any that keep to these rules, and one draw needn't show every extreme that they name: `seg_owner`: in each device's block of 128 segments no owner appears more than 8 times; one owner device receives exactly 8 segments from every device's block.
All inputs are finite; a program needn't handle non-finite values.
Results may differ from a plain program's by a relative error of at most 0.006.
Values may be sent and summed in bfloat16 or wider, within the bound.
A program may use at most 64 MiB of HBM per device.

v0:
```python
import functools

import jax
import jax.numpy as jnp
import numpy as np
from jax import lax
from jax.experimental import pallas as pl
from jax.experimental.pallas import tpu as pltpu
from jax.sharding import PartitionSpec as P

ELEM_NODES = 64
LANES = 128
FACE = 16
VMEM_LIMIT = 56 * 1024 * 1024
NT = (((1,), (1,)), ((), ()))
NN = (((1,), (0,)), ((), ()))


def face_nodes():
    node_rows = []
    for side_idx in range(6):
        normal_axis = side_idx // 2
        plane_level = 3 * (side_idx % 2)
        row_nodes = []
        for first_coord in range(4):
            for second_coord in range(4):
                position = [first_coord, second_coord]
                position.insert(normal_axis, plane_level)
                row_nodes.append(16 * position[0] + 4 * position[1] + position[2])
        node_rows.append(row_nodes)
    return np.array(node_rows, dtype=np.int32)


def side_nodes(side_ids):
    node_table = jnp.asarray(face_nodes())
    side_hot = (side_ids[:, None] == jnp.arange(6, dtype=jnp.int32)[None, :]).astype(jnp.int32)
    return jnp.sum(side_hot[:, :, None] * node_table[None, :, :], axis=1)


def mm(a, b, dims=NN):
    return lax.dot_general(a, b, dims, preferred_element_type=jnp.float32)


def iota(shape, dim):
    return lax.broadcasted_iota(jnp.int32, shape, dim)


def hot(mask):
    return jnp.where(mask, 1.0, 0.0).astype(jnp.bfloat16)


def perm_hot(shape, chaos_dim, wide_dim, part, padded):
    i = iota(shape, chaos_dim)
    return hot(iota(shape, wide_dim) == i // part * padded + i % part)


def block_diag(flat):
    spread = mm(hot(iota((LANES, 8), 0) // FACE == iota((LANES, 8), 1)), flat)
    own_row = iota((LANES, 256), 1) // FACE == iota((LANES, 256), 0) % FACE
    spread = jnp.where(own_row, spread, 0.0).astype(jnp.bfloat16)
    fold = hot(iota((256, LANES), 0) % FACE == iota((256, LANES), 1) % FACE)
    tiled = mm(spread, fold)
    same = iota((LANES, LANES), 0) // FACE == iota((LANES, LANES), 1) // FACE
    return jnp.where(same, tiled, 0.0).astype(jnp.bfloat16)


def node_hot(target_row):
    return hot(iota((8 * LANES, LANES), 0) == target_row)


def faces_of(fp_ref, pair_ref, group):
    return jnp.concatenate([fp_ref[pair_ref[group * 8 + j]] for j in range(8)], axis=1)


def weave_kernel(mort_ref, target_ref, out_ref):
    for h in range(out_ref.shape[0]):
        mats = block_diag(mort_ref[h])
        out_ref[h] = mm(mats, node_hot(target_ref[h]), NT).astype(jnp.bfloat16)


def tail_hot(shape, dense_dim, low):
    dense, row = iota(shape, dense_dim), iota(shape, 1 - dense_dim)
    return hot((row // 16 == dense // low) & (row % 16 == dense % low))


def send_kernel(field_ref, out_ref):
    part, nodes = field_ref.shape
    high = part // 16 * 16
    low, width = part - high, nodes // 16
    total = jnp.zeros((16 * low, width), jnp.float32)
    for q in range(16):
        cols = slice(q * width, (q + 1) * width)
        out_ref[0, q * high:(q + 1) * high, :] = field_ref[:high, cols]
        shape = (16 * low, low)
        place = hot(iota(shape, 0) == q * low + iota(shape, 1))
        total = total + mm(place, field_ref[high:part, cols])
    out_ref[0, 16 * high:, :] = total.astype(jnp.bfloat16)


def receive_kernel(in_ref, out_ref):
    part, nodes = out_ref.shape
    high = part // 16 * 16
    low, width = part - high, nodes // 16
    tail = in_ref[0, 16 * high:, :]
    for q in range(16):
        cols = slice(q * width, (q + 1) * width)
        out_ref[:high, cols] = in_ref[0, q * high:(q + 1) * high, :]
        shape = (low, 16 * low)
        pick = hot(iota(shape, 1) == q * low + iota(shape, 0))
        out_ref[high:part, cols] = mm(pick, tail).astype(jnp.bfloat16)


def pack_kernel(owner_col_ref, owner_row_ref, die_ref, int_ref, small_ref, die_out, meta_out, small_out, *, cap):
    segs = owner_row_ref.shape[1]
    slots = die_out.shape[0]
    same = owner_col_ref[...] == owner_row_ref[...]
    before = iota((segs, segs), 0) < iota((segs, segs), 1)
    rank = jnp.sum(jnp.where(same & before, 1.0, 0.0), axis=0, keepdims=True).astype(jnp.int32)
    place = hot(iota((slots, segs), 0) == owner_row_ref[...] * cap + rank)
    die_out[...] = mm(place, die_ref[...]).astype(jnp.bfloat16)
    small = mm(place, small_ref[...])
    small_out[...] = small
    meta_out[:, :256] = mm(place, int_ref[...]).astype(jnp.bfloat16)
    meta_out[:, 256:] = small.astype(jnp.bfloat16)


def unpack(wide_ref, fp_out, part):
    n_chaos, rows, width = wide_ref.shape
    high = part // 16 * 16
    low = part - high
    padded = high + 16
    spread = tail_hot((256, 16 * low), 1, low)
    tails = [mm(spread, wide_ref[c, 16 * high:, :]).astype(jnp.bfloat16) for c in range(n_chaos)]
    perm = perm_hot((part * n_chaos, padded * n_chaos), 0, 1, part, padded)
    per = width // LANES
    for q in range(16):
        pieces = []
        for c in range(n_chaos):
            pieces.append(wide_ref[c, q * high:(q + 1) * high, :])
            pieces.append(tails[c][q * 16:(q + 1) * 16])
        block = mm(perm, jnp.concatenate(pieces, axis=0)).astype(jnp.bfloat16)
        for h in range(per):
            fp_out[q * per + h] = block[:, h * LANES:(h + 1) * LANES]


def project_kernel(pair_ref, wide_ref, weave_ref, fp_out, proj_out, *, part):
    step = pl.program_id(0)

    @pl.when(step == 0)
    def _():
        unpack(wide_ref, fp_out, part)

    for h in range(proj_out.shape[0]):
        face = faces_of(fp_out, pair_ref, step * proj_out.shape[0] + h)
        proj_out[h] = mm(face, weave_ref[h], NT).astype(jnp.bfloat16)


def own_project_kernel(pair_ref, fp_ref, weave_ref, proj_out):
    for h in range(proj_out.shape[0]):
        face = faces_of(fp_ref, pair_ref, pl.program_id(0) * proj_out.shape[0] + h)
        proj_out[h] = mm(face, weave_ref[h], NT)


def mix(coupling_ref, block, weights):
    total = weights[0:1] * block.astype(jnp.float32)
    for k in range(coupling_ref.shape[0]):
        total = total + weights[k + 1:k + 2] * mm(coupling_ref[k], block)
    return total.astype(jnp.bfloat16)


def element_kernel(fp_ref, coupling_ref, kl_ref, stiff_ref, out_ref):
    def step(p, carry):
        block = jnp.concatenate([fp_ref[2 * p], fp_ref[2 * p + 1]], axis=1)
        mixed = mix(coupling_ref, block, kl_ref[p])
        out_ref[2 * p] = mm(mixed[:, :LANES], stiff_ref[2 * p], NT)
        out_ref[2 * p + 1] = mm(mixed[:, LANES:], stiff_ref[2 * p + 1], NT)
        return carry

    lax.fori_loop(0, fp_ref.shape[0] // 2, step, 0)


def flux_kernel(recv_ref, own_ref, coupling_ref, coef_ref, flux_out):
    def step(p, carry):
        jump = [
            (recv_ref[2 * p + h].astype(jnp.float32) - own_ref[2 * p + h]).astype(jnp.bfloat16)
            for h in range(2)
        ]
        flux = mix(coupling_ref, jnp.concatenate(jump, axis=1), coef_ref[p])
        flux_out[2 * p] = flux[:, :LANES]
        flux_out[2 * p + 1] = flux[:, LANES:]
        return carry

    lax.fori_loop(0, recv_ref.shape[0] // 2, step, 0)


def scatter_step(pair_ref, flux_ref, weave_ref, acc_ref, sign):
    for h in range(flux_ref.shape[0]):
        back = mm(flux_ref[h], weave_ref[h])
        for j in range(8):
            pair = pair_ref[(pl.program_id(0) * flux_ref.shape[0] + h) * 8 + j]
            acc_ref[pair] = acc_ref[pair] + sign * back[:, j * LANES:(j + 1) * LANES]


def own_back_kernel(pair_ref, flux_ref, weave_ref, start_ref, acc_out):
    @pl.when(pl.program_id(0) == 0)
    def _():
        acc_out[...] = start_ref[...]

    scatter_step(pair_ref, flux_ref, weave_ref, acc_out, -1.0)


def die_back_kernel(pair_ref, flux_ref, weave_ref, start_ref, out_ref, acc_ref, tail_ref, *, part):
    @pl.when(pl.program_id(0) == 0)
    def _():
        acc_ref[...] = start_ref[...]

    scatter_step(pair_ref, flux_ref, weave_ref, acc_ref, 1.0)

    @pl.when(pl.program_id(0) == pl.num_programs(0) - 1)
    def _():
        n_chaos, rows, width = out_ref.shape
        high = part // 16 * 16
        low = part - high
        padded = high + 16
        perm = perm_hot((padded * n_chaos, part * n_chaos), 1, 0, part, padded)
        per = width // LANES
        for q in range(16):
            block = jnp.concatenate([acc_ref[q * per + h].astype(jnp.bfloat16) for h in range(per)], axis=1)
            block = mm(perm, block).astype(jnp.bfloat16)
            for c in range(n_chaos):
                out_ref[c, q * high:(q + 1) * high, :] = block[c * padded:c * padded + high]
                tail_ref[c, q * 16:(q + 1) * 16, :] = block[c * padded + high:(c + 1) * padded]
        gather = tail_hot((16 * low, 256), 0, low)
        for c in range(n_chaos):
            out_ref[c, 16 * high:, :] = mm(gather, tail_ref[c]).astype(jnp.bfloat16)


def call(kernel, outs, args, scalars=0, scratch=(), steps=0, split=(), split_outs=()):
    many = isinstance(outs, tuple)
    shapes = outs if many else (outs,)

    def spec(shape, cut):
        if steps == 0:
            return pl.BlockSpec(memory_space=pltpu.VMEM)
        rest = (0,) * (len(shape) - 1)
        if cut:
            return pl.BlockSpec((shape[0] // steps,) + tuple(shape[1:]), lambda i: (i,) + rest)
        return pl.BlockSpec(tuple(shape), lambda i: (0,) + rest)

    in_specs = [
        pl.BlockSpec(memory_space=pltpu.SMEM) if n < scalars else spec(x.shape, n in split)
        for n, x in enumerate(args)
    ]
    out_specs = tuple(spec(x.shape, n in split_outs) for n, x in enumerate(shapes))
    moved = sum(x.size * x.dtype.itemsize for x in (*args, *shapes))
    result = pl.pallas_call(
        kernel,
        out_shape=shapes,
        grid=(steps,) if steps else (),
        in_specs=in_specs,
        out_specs=out_specs,
        scratch_shapes=scratch,
        compiler_params=pltpu.CompilerParams(vmem_limit_bytes=VMEM_LIMIT),
        cost_estimate=pl.CostEstimate(flops=0, bytes_accessed=moved, transcendentals=0),
    )(*args)
    return result if many else result[0]


def dense_coupling(triple_mode, triple_row, triple_col, triple_value, mode_count, chaos_width):
    flat_index = triple_mode * chaos_width + triple_row
    left_hot = (
        flat_index[:, None] == jnp.arange(mode_count * chaos_width, dtype=jnp.int32)[None, :]
    ).astype(jnp.float32)
    right_hot = (triple_col[:, None] == jnp.arange(chaos_width, dtype=jnp.int32)[None, :]).astype(
        jnp.float32
    ) * triple_value[:, None]
    summed = jnp.einsum(
        "ta,tb->ab",
        left_hot,
        right_hot,
        precision=lax.Precision.HIGHEST,
        preferred_element_type=jnp.float32,
    )
    return summed.reshape(mode_count, chaos_width, chaos_width).astype(jnp.bfloat16)


def slot_targets(elem, side):
    slots = elem.shape[0]
    lane_block = (jnp.arange(slots, dtype=jnp.int32) % 8) * LANES + (elem % 2) * ELEM_NODES
    target = lane_block[:, None] + side_nodes(side)
    return elem // 2, target.reshape(slots // 8, 1, LANES)


def lane_weights(rows, repeat):
    rows = jnp.pad(rows, ((0, 16 - rows.shape[0]), (0, 0)))
    per = 256 // repeat
    tiles = rows.shape[1] // per
    rows = jnp.transpose(rows.reshape(16, tiles, per), (1, 0, 2))
    spread = (jnp.arange(per)[:, None] == jnp.arange(256)[None, :] // repeat).astype(jnp.float32)
    return jnp.einsum("tkp,pl->tkl", rows, spread, precision=lax.Precision.HIGHEST)


def local(
    field,
    stiffness,
    kl_coef,
    triple_mode,
    triple_row,
    triple_col,
    triple_value,
    die_elem,
    die_side,
    seg_owner,
    seg_face,
    die_mortar,
    int_mortar,
    bump_coef,
    int_elem,
    int_side,
):
    n_chaos = lax.axis_size("chaos")
    devices = lax.axis_size("space") * n_chaos
    part, local_nodes = field.shape
    chaos = part * n_chaos
    nodes = local_nodes // n_chaos
    segs = die_elem.shape[0]
    cap = max(2, 2 * segs // devices)
    slots = devices * cap
    groups = slots // 8
    pairs = nodes // LANES
    modes = bump_coef.shape[1] - 1
    bf16, f32 = jnp.bfloat16, jnp.float32
    axes = ("space", "chaos")

    sent = pl.pallas_call(
        send_kernel,
        out_shape=jax.ShapeDtypeStruct((n_chaos, 16 * part, nodes // 16), bf16),
        grid=(n_chaos,),
        in_specs=[pl.BlockSpec((part, nodes), lambda c: (0, c))],
        out_specs=pl.BlockSpec((1, 16 * part, nodes // 16), lambda c: (c, 0, 0)),
    )(field)
    wide = lax.all_to_all(sent, "chaos", split_axis=0, concat_axis=0, tiled=True)

    ints = jnp.stack([seg_face, die_elem, die_side], axis=1).astype(bf16)
    small = jnp.pad(jnp.concatenate([bump_coef, ints], axis=1), ((0, 0), (0, LANES - modes - 4)))
    die_slots, meta, small_slots = call(
        functools.partial(pack_kernel, cap=cap),
        (
            jax.ShapeDtypeStruct((slots, 256), bf16),
            jax.ShapeDtypeStruct((slots, 256 + LANES), bf16),
            jax.ShapeDtypeStruct((slots, LANES), f32),
        ),
        (seg_owner[:, None], seg_owner[None, :], die_mortar, int_mortar, small),
    )
    die_ids = small_slots[:, modes + 2:modes + 4].astype(jnp.int32)
    die_pair, die_target = slot_targets(die_ids[:, 0], die_ids[:, 1])

    coupling = dense_coupling(triple_mode, triple_row, triple_col, triple_value, modes, chaos)
    groups3 = (groups, 8, 256)
    weave_shape = jax.ShapeDtypeStruct((groups, LANES, 8 * LANES), bf16)
    steps = groups // 4
    die_weave = call(
        weave_kernel,
        weave_shape,
        (die_slots.reshape(groups3), die_target),
        steps=steps,
        split=(0, 1),
        split_outs=(0,),
    )
    wide, meta, die_weave, die_pair, coupling = lax.optimization_barrier(
        (wide, meta, die_weave, die_pair, coupling)
    )
    meta = lax.all_to_all(meta, axes, split_axis=0, concat_axis=0, tiled=True)
    fp, proj = call(
        functools.partial(project_kernel, part=part),
        (
            jax.ShapeDtypeStruct((pairs, chaos, LANES), bf16),
            jax.ShapeDtypeStruct((groups, chaos, LANES), bf16),
        ),
        (die_pair, wide, die_weave),
        1,
        steps=steps,
        split=(2,),
        split_outs=(1,),
    )

    meta, proj = lax.optimization_barrier((meta, proj))

    def exchange(values):
        per = devices // groups
        values = values.reshape(groups, chaos, per, LANES // per)
        values = jnp.transpose(values, (0, 2, 1, 3)).reshape(devices, chaos, LANES // per)
        values = lax.all_to_all(values, axes, split_axis=0, concat_axis=0, tiled=True)
        values = values.reshape(groups, per, chaos, LANES // per)
        return jnp.transpose(values, (0, 2, 1, 3)).reshape(groups, chaos, LANES)

    recv = exchange(proj)

    int_slots = meta[:, :256]
    recv_small = meta[:, 256:256 + modes + 2].astype(f32)
    coef_lanes = lane_weights(recv_small[:, :modes + 1].T, FACE)
    face_hot = recv_small[:, modes + 1].astype(jnp.int32)[:, None] == jnp.arange(int_elem.shape[0])[None, :]
    own_elem = jnp.sum(jnp.where(face_hot, int_elem[None, :], 0), axis=1)
    own_side = jnp.sum(jnp.where(face_hot, int_side[None, :], 0), axis=1)
    own_pair, own_target = slot_targets(own_elem, own_side)

    int_weave = call(
        weave_kernel,
        weave_shape,
        (int_slots.reshape(groups3), own_target),
        steps=steps,
        split=(0, 1),
        split_outs=(0,),
    )
    own_proj = call(
        own_project_kernel,
        jax.ShapeDtypeStruct((groups, chaos, LANES), f32),
        (own_pair, fp, int_weave),
        1,
        steps=steps,
        split=(2,),
        split_outs=(0,),
    )
    flux = call(
        flux_kernel,
        jax.ShapeDtypeStruct((groups, chaos, LANES), bf16),
        (recv, own_proj, coupling, coef_lanes),
    )
    flux, stiffness, kl_coef = lax.optimization_barrier((flux, stiffness, kl_coef))
    back_flux = exchange(flux)
    kl_lanes = lane_weights(kl_coef, ELEM_NODES)
    blocks = stiffness.reshape(pairs, 2, ELEM_NODES, 1, ELEM_NODES)
    on_diag = jnp.eye(2, dtype=bool)[None, :, None, :, None]
    stiff = jnp.where(on_diag, blocks, jnp.zeros((), bf16)).reshape(pairs, LANES, LANES)
    local_out = call(
        element_kernel,
        jax.ShapeDtypeStruct((pairs, chaos, LANES), f32),
        (fp, coupling, kl_lanes, stiff),
    )
    local_out = call(
        own_back_kernel,
        jax.ShapeDtypeStruct((pairs, chaos, LANES), f32),
        (own_pair, flux, int_weave, local_out),
        1,
        steps=steps,
        split=(1, 2),
    )
    result = call(
        functools.partial(die_back_kernel, part=part),
        jax.ShapeDtypeStruct(sent.shape, bf16),
        (die_pair, back_flux, die_weave, local_out),
        1,
        (
            pltpu.VMEM((pairs, chaos, LANES), f32),
            pltpu.VMEM((n_chaos, 256, nodes // 16), bf16),
        ),
        steps=steps,
        split=(1, 2),
    )
    returned = lax.all_to_all(result, "chaos", split_axis=0, concat_axis=0, tiled=True)
    return pl.pallas_call(
        receive_kernel,
        out_shape=jax.ShapeDtypeStruct((part, local_nodes), bf16),
        grid=(n_chaos,),
        in_specs=[pl.BlockSpec((1, 16 * part, nodes // 16), lambda c: (c, 0, 0))],
        out_specs=pl.BlockSpec((part, nodes), lambda c: (0, c)),
    )(returned)


def solution(mesh):
    in_specs = (
        P("chaos", "space"),
        P(("space", "chaos"), None),
        P(None, ("space", "chaos")),
        P(),
        P(),
        P(),
        P(),
        P(("space", "chaos")),
        P(("space", "chaos")),
        P(("space", "chaos")),
        P(("space", "chaos")),
        P(("space", "chaos"), None),
        P(("space", "chaos"), None),
        P(("space", "chaos"), None),
        P(("space", "chaos")),
        P(("space", "chaos")),
    )
    out_specs = P("chaos", "space")
    return jax.shard_map(local, mesh=mesh, in_specs=in_specs, out_specs=out_specs, check_vma=False)
```

profile of v0, /device:TPU:0, one launch (start us, length us, event | category | flops | bytes accessed | tf_op | source)
XLA Modules:
  0.0 198.1 jit_solution(2686896206816429078)
XLA Ops:
  0.0 0.0 copy-start.9
  0.0 4.5 %shard_map.172 = bf16[4,672,256]{2,1,0:T(8,128)(2,1)} custom-call(bf16[42,16384]{1,0:T(8,128)(2,1)} %field_ref.1), custom_call_target="tpu_custom_call" | custom-call | tf_op jit(solution)/shard_map/pallas_call | solution.py:335
  4.5 6.5 %all-to-all-start = ((bf16[4,672,256]{2,1,0:T(8,128)(2,1)}), bf16[4,672,256]{2,1,0:T(8,128)(2,1)S(1)}, u32[]{:S(2)}, u32[]{:S(2)}) async-start(bf16[4,672,256]{2,1,0:T(8,128)(2,1)} %shard_map.172), calls=%async_computation | async-start | bytes 2752512 | tf_op jit(solution)/shard_map/all_to_all | solution.py:342
  11.0 0.0 copy-done.11
  11.0 0.0 copy-done.10
  11.1 0.1 copy.83
  11.2 0.7 copy.84.owner_col_ref
  11.9 0.6 pad.12.small_ref
  12.6 2.0 shard_map.173
  14.5 1.0 slice_convert_fusion.1
  15.6 0.2 slice_reduce_fusion.1
  15.8 0.1 multiply_reduce_fusion.1
  15.9 0.1 copy.86
  16.0 0.1 reduce_sum.43
  16.1 0.1 add.107
  16.2 0.1 copy.85
  16.3 0.1 copy.87
  16.3 0.0 copy-done.5
  16.4 0.0 copy-done.14
  16.4 0.0 copy-done.15
  16.4 6.9 %fusion.3 = bf16[1344,168]{0,1:T(8,128)(2,1)S(1)} fusion(s32[2688]{0:T(1024)S(1)} %multiply_add_fusion, f32[2688]{0:T(1024)S(1)} %copy-done.14, s32[2688]{0:T(1024)S(1)} %copy-done.15), kind=kOutput, calls=%fused_computation.5 | convolution fusion | flops 7287888384 | bytes 483840 | tf_op jit(solution)/shard_map/ta,tb->ab/dot_general | solution.py:277
  23.3 1.2 copy.89
  24.5 0.6 add.110
  25.1 13.1 %shard_map.174.weave_ref = bf16[32,128,1024]{2,1,0:T(8,128)(2,1)} custom-call(bf16[32,8,256]{2,1,0:T(8,128)(2,1)} %bitcast.41, s32[32,1,128]{2,1,0:T(1,128)} %bitcast.44), custom_call_target="tpu_custom_call" | custom-call | bytes 8536064 | tf_op jit(solution)/shard_map/pallas_call | solution.py:256
  38.2 0.6 and_select_fusion.3.pair_ref
  38.8 4.9 %all-to-all-done.wide_ref = bf16[4,672,256]{2,1,0:T(8,128)(2,1)S(1)} async-done(((bf16[4,672,256]{2,1,0:T(8,128)(2,1)}), bf16[4,672,256]{2,1,0:T(8,128)(2,1)S(1)}, u32[]{:S(2)}, u32[]{:S(2)}) %all-to-all-start) | async-done | bytes 1376288 | tf_op jit(solution)/shard_map/all_to_all | solution.py:342
  43.7 3.7 %all-to-all-start.1 = ((bf16[32,8,384]{2,1,0:T(8,128)(2,1)}), bf16[32,8,384]{2,1,0:T(8,128)(2,1)S(1)}, u32[]{:S(2)}, u32[]{:S(2)}) async-start(bf16[32,8,384]{2,1,0:T(8,128)(2,1)} %bitcast.9), calls=%async_computation.1 | async-start | bytes 393216 | tf_op jit(solution)/shard_map/all_to_all | solution.py:373
  47.5 10.4 %shard_map.175 = (bf16[32,168,128]{2,1,0:T(8,128)(2,1)}, bf16[32,168,128]{2,1,0:T(8,128)(2,1)}) custom-call(s32[256]{0:T(256)} %and_select_fusion.3.pair_ref, bf16[4,672,256]{2,1,0:T(8,128)(2,1)} %copy-done, bf16[32,128,1024]{2,1,0:T(8,128)(2,1)} %shard_map.174.weave_ref), custom_call_target="tpu_custom_call" | custom-call | bytes 12518400 | tf_op jit(solution)/shard_map/pallas_call | solution.py:256
  57.9 0.0 all-to-all-done.1
  57.9 6.0 %all-to-all-start.2 = ((bf16[32,168,128]{2,1,0:T(8,128)(2,1)}), bf16[32,168,128]{2,1,0:T(8,128)(2,1)S(1)}, u32[]{:S(2)}, u32[]{:S(2)}) async-start(bf16[32,168,128]{2,1,0:T(8,128)(2,1)} %get-tuple-element.28), calls=%async_computation.2 | async-start | bytes 2752512 | tf_op jit(solution)/shard_map/all_to_all | solution.py:393
  63.9 0.2 fusion.14
  64.1 0.1 select_reduce_fusion
  64.2 0.1 reduce_sum.45
  64.3 0.1 copy.90
  64.4 0.1 copy.94
  64.5 0.1 multiply_reduce_fusion
  64.6 0.1 copy.93
  64.7 0.1 reduce_sum.48
  64.8 0.1 copy.97
  64.9 0.6 add.117
  65.5 0.7 slice_bitcast_fusion.1.mort_ref
  66.2 13.1 %shard_map.176.weave_ref = bf16[32,128,1024]{2,1,0:T(8,128)(2,1)} custom-call(bf16[32,8,256]{2,1,0:T(8,128)(2,1)} %slice_bitcast_fusion.1.mort_ref, s32[32,1,128]{2,1,0:T(1,128)} %bitcast.43), custom_call_target="tpu_custom_call" | custom-call | bytes 8536064 | tf_op jit(solution)/shard_map/pallas_call | solution.py:256
  79.3 0.6 and_select_fusion.2.pair_ref
  79.9 9.6 %shard_map.177.own_ref = f32[32,168,128]{2,1,0:T(8,128)} custom-call(s32[256]{0:T(256)} %and_select_fusion.2.pair_ref, bf16[32,168,128]{2,1,0:T(8,128)(2,1)} %get-tuple-element.30.fp_ref, bf16[32,128,1024]{2,1,0:T(8,128)(2,1)} %shard_map.176.weave_ref), custom_call_target="tpu_custom_call" | custom-call | bytes 12518400 | tf_op jit(solution)/shard_map/pallas_call | solution.py:256
  89.5 0.9 fusion.15.coef_ref
  90.4 5.2 %all-to-all-done.2.recv_ref = bf16[32,168,128]{2,1,0:T(8,128)(2,1)S(1)} async-done(((bf16[32,168,128]{2,1,0:T(8,128)(2,1)}), bf16[32,168,128]{2,1,0:T(8,128)(2,1)S(1)}, u32[]{:S(2)}, u32[]{:S(2)}) %all-to-all-start.2) | async-done | bytes 1376288 | tf_op jit(solution)/shard_map/all_to_all | solution.py:393
  95.6 1.1 copy-done.1
  96.7 9.1 %shard_map.178.flux_ref = bf16[32,168,128]{2,1,0:T(8,128)(2,1)} custom-call(bf16[32,168,128]{2,1,0:T(8,128)(2,1)} %copy-done.1, f32[32,168,128]{2,1,0:T(8,128)} %shard_map.177.own_ref, bf16[8,168,168]{2,1,0:T(8,128)(2,1)} %bitcast.34, f32[16,16,256]{2,1,0:T(8,128)} %fusion.15.coef_ref), custom_call_target="tpu_custom_call" | custom-call | bytes 6218752 | tf_op jit(solution)/shard_map/pallas_call | solution.py:256
  105.8 4.6 %all-to-all-start.3 = ((bf16[32,168,128]{2,1,0:T(8,128)(2,1)}), bf16[32,168,128]{2,1,0:T(8,128)(2,1)S(1)}, u32[]{:S(2)}, u32[]{:S(2)}) async-start(bf16[32,168,128]{2,1,0:T(8,128)(2,1)} %shard_map.178.flux_ref), calls=%async_computation.3 | async-start | bytes 2752512 | tf_op jit(solution)/shard_map/all_to_all | solution.py:393
  110.4 0.1 broadcast_in_dim.80
  110.5 0.1 broadcast_in_dim.81
  110.6 2.1 %broadcast_in_dim.83 = bf16[32,2,64,64]{3,2,1,0:T(8,128)(2,1)} reshape(bf16[64,4096]{1,0:T(8,128)(2,1)S(1)} %copy-done.3) | data formatting | bytes 1048576 | tf_op jit(solution)/shard_map/jit(_where)/broadcast_in_dim | solution.py:434
  112.7 3.3 %broadcast_in_dim.84 = bf16[32,2,64,2,64]{4,3,2,1,0:T(2,128)(2,1)S(1)} broadcast(bf16[32,2,64,64]{3,2,1,0:T(8,128)(2,1)} %broadcast_in_dim.83), dimensions={0,1,2,4} | broadcast | bytes 1572864 | tf_op jit(solution)/shard_map/jit(_where)/broadcast_in_dim | solution.py:434
  116.0 1.8 broadcast_in_dim.85
  117.8 0.1 copy.101
  117.9 1.1 fusion.33.kl_ref
  118.9 2.3 %broadcast_select_fusion.stiff_ref = bf16[32,128,128]{2,1,0:T(8,128)(2,1)} fusion(bf16[32,128,128]{2,1,0:T(8,128)(2,1)} %broadcast_in_dim.85, pred[128,128]{1,0:T(8,128)(4,1)S(1)} %broadcast_in_dim.81), kind=kLoop, calls=%fused_computation.9 | loop fusion | flops 524288 | bytes 2113536 | tf_op jit(solution)/shard_map/jit(_where)/select_n | solution.py:434
  121.2 11.2 %shard_map.179.start_ref = f32[32,168,128]{2,1,0:T(8,128)} custom-call(bf16[32,168,128]{2,1,0:T(8,128)(2,1)} %get-tuple-element.30.fp_ref, bf16[8,168,168]{2,1,0:T(8,128)(2,1)} %bitcast.35, f32[16,16,256]{2,1,0:T(8,128)} %fusion.33.kl_ref, bf16[32,128,128]{2,1,0:T(8,128)(2,1)} %broadcast_select_fusion.stiff_ref), custom_call_target="tpu_custom_call" | custom-call | bytes 5891072 | tf_op jit(solution)/shard_map/pallas_call | solution.py:256
  132.4 11.1 %shard_map.180.start_ref = f32[32,168,128]{2,1,0:T(8,128)} custom-call(s32[256]{0:T(256)} %and_select_fusion.2.pair_ref, bf16[32,168,128]{2,1,0:T(8,128)(2,1)} %shard_map.178.flux_ref, bf16[32,128,1024]{2,1,0:T(8,128)(2,1)} %shard_map.176.weave_ref, f32[32,168,128]{2,1,0:T(8,128)} %shard_map.179.start_ref), custom_call_target="tpu_custom_call" | custom-call | bytes 15270912 | tf_op jit(solution)/shard_map/pallas_call | solution.py:256
  143.5 0.0 all-to-all-done.3.flux_ref
  143.5 1.1 copy-done.2
  144.6 11.4 %shard_map.181 = bf16[4,672,256]{2,1,0:T(8,128)(2,1)} custom-call(s32[256]{0:T(256)} %and_select_fusion.3.pair_ref, bf16[32,168,128]{2,1,0:T(8,128)(2,1)} %copy-done.2, bf16[32,128,1024]{2,1,0:T(8,128)(2,1)} %shard_map.174.weave_ref, f32[32,168,128]{2,1,0:T(8,128)} %shard_map.180.start_ref), custom_call_target="tpu_custom_call" | custom-call | bytes 13894656 | tf_op jit(solution)/shard_map/pallas_call | solution.py:256
  156.0 38.0 %all_to_all.32.in_ref = bf16[4,672,256]{2,1,0:T(8,128)(2,1)} all-to-all(bf16[4,672,256]{2,1,0:T(8,128)(2,1)} %shard_map.181), channel_id=1, replica_groups=mesh['space'=8,'chaos'=4] {'chaos'}, dimensions={0} | all-to-all | bytes 2752512 | tf_op jit(solution)/shard_map/all_to_all | solution.py:460
  194.0 4.0 %shard_map.182 = bf16[42,16384]{1,0:T(8,128)(2,1)} custom-call(bf16[4,672,256]{2,1,0:T(8,128)(2,1)} %all_to_all.32.in_ref), custom_call_target="tpu_custom_call" | custom-call | tf_op jit(solution)/shard_map/pallas_call | solution.py:461
  (42 shorter events, 0.2 us)
Async XLA Ops:
  0.0 15.8 %copy-start.4 = (s32[6,16]{1,0:T(8,128)S(1)}, s32[6,16]{1,0:T(8,128)}, u32[]{:S(2)}) copy-start(s32[6,16]{1,0:T(8,128)} %constant.97.clone) | copy-start | bytes 1156
  0.0 11.0 %copy-start.16 = (s32[128]{0:T(128)S(1)}, s32[128]{0:T(128)}, u32[]{:S(2)}) copy-start(s32[128]{0:T(128)} %param.28) | copy-start | bytes 1540
  0.0 11.0 %copy-start.11 = (s32[128]{0:T(128)S(1)}, s32[128]{0:T(128)}, u32[]{:S(2)}) copy-start(s32[128]{0:T(128)} %param.25) | copy-start | bytes 1540
  0.0 11.0 %copy-start.10 = (s32[128]{0:T(128)S(1)}, s32[128]{0:T(128)}, u32[]{:S(2)}) copy-start(s32[128]{0:T(128)} %param.26) | copy-start | bytes 1540
  0.0 11.0 %copy-start.8 = (bf16[128,9]{0,1:T(8,128)(2,1)S(1)}, bf16[128,9]{0,1:T(8,128)(2,1)}, u32[]{:S(2)}) copy-start(bf16[128,9]{0,1:T(8,128)(2,1)} %param.31) | copy-start | bytes 6916
  0.0 11.2 %copy-start.9 = (s32[128]{0:T(128)S(1)}, s32[128]{0:T(128)}, u32[]{:S(2)}) copy-start(s32[128]{0:T(128)} %param.27) | copy-start | bytes 1540
  4.5 11.8 %copy-start.5 = (s32[2688]{0:T(1024)S(1)}, s32[2688]{0:T(1024)}, u32[]{:S(2)}) copy-start(s32[2688]{0:T(1024)} %param.22) | copy-start | bytes 32260
  4.5 11.8 %copy-start.6 = (s32[2688]{0:T(1024)S(1)}, s32[2688]{0:T(1024)}, u32[]{:S(2)}) copy-start(s32[2688]{0:T(1024)} %param.21) | copy-start | bytes 32260
  4.5 11.8 %copy-start.14 = (f32[2688]{0:T(1024)S(1)}, f32[2688]{0:T(1024)}, u32[]{:S(2)}) copy-start(f32[2688]{0:T(1024)} %param.24) | copy-start | bytes 32260
  4.5 11.9 %copy-start.15 = (s32[2688]{0:T(1024)S(1)}, s32[2688]{0:T(1024)}, u32[]{:S(2)}) copy-start(s32[2688]{0:T(1024)} %param.23) | copy-start | bytes 32260
  4.5 39.2 %all-to-all-start = ((bf16[4,672,256]{2,1,0:T(8,128)(2,1)}), bf16[4,672,256]{2,1,0:T(8,128)(2,1)S(1)}, u32[]{:S(2)}, u32[]{:S(2)}) async-start(bf16[4,672,256]{2,1,0:T(8,128)(2,1)} %shard_map.172), calls=%async_computation | async-start | bytes 2752512 | tf_op jit(solution)/shard_map/all_to_all | solution.py:342
  43.7 3.7 %copy-start = (bf16[4,672,256]{2,1,0:T(8,128)(2,1)}, bf16[4,672,256]{2,1,0:T(8,128)(2,1)S(1)}, u32[]{:S(2)}) copy-start(bf16[4,672,256]{2,1,0:T(8,128)(2,1)S(1)} %all-to-all-done.wide_ref) | copy-start | bytes 4128772
  43.7 14.1 %all-to-all-start.1 = ((bf16[32,8,384]{2,1,0:T(8,128)(2,1)}), bf16[32,8,384]{2,1,0:T(8,128)(2,1)S(1)}, u32[]{:S(2)}, u32[]{:S(2)}) async-start(bf16[32,8,384]{2,1,0:T(8,128)(2,1)} %bitcast.9), calls=%async_computation.1 | async-start | bytes 393216 | tf_op jit(solution)/shard_map/all_to_all | solution.py:373
  57.9 6.3 %copy-start.12 = (s32[64]{0:T(128)S(1)}, s32[64]{0:T(128)}, u32[]{:S(2)}) copy-start(s32[64]{0:T(128)} %param.33) | copy-start | bytes 772
  57.9 6.3 %copy-start.13 = (s32[64]{0:T(128)S(1)}, s32[64]{0:T(128)}, u32[]{:S(2)}) copy-start(s32[64]{0:T(128)} %param.32) | copy-start | bytes 772
  57.9 37.7 %all-to-all-start.2 = ((bf16[32,168,128]{2,1,0:T(8,128)(2,1)}), bf16[32,168,128]{2,1,0:T(8,128)(2,1)S(1)}, u32[]{:S(2)}, u32[]{:S(2)}) async-start(bf16[32,168,128]{2,1,0:T(8,128)(2,1)} %get-tuple-element.28), calls=%async_computation.2 | async-start | bytes 2752512 | tf_op jit(solution)/shard_map/all_to_all | solution.py:393
  95.6 1.1 copy-start.1
  105.8 4.8 %copy-start.3 = (bf16[64,4096]{1,0:T(8,128)(2,1)S(1)}, bf16[64,4096]{1,0:T(8,128)(2,1)}, u32[]{:S(2)}) copy-start(bf16[64,4096]{1,0:T(8,128)(2,1)} %param.19) | copy-start | bytes 1572868
  105.8 37.7 %all-to-all-start.3 = ((bf16[32,168,128]{2,1,0:T(8,128)(2,1)}), bf16[32,168,128]{2,1,0:T(8,128)(2,1)S(1)}, u32[]{:S(2)}, u32[]{:S(2)}) async-start(bf16[32,168,128]{2,1,0:T(8,128)(2,1)} %shard_map.178.flux_ref), calls=%async_computation.3 | async-start | bytes 2752512 | tf_op jit(solution)/shard_map/all_to_all | solution.py:393
  112.7 5.1 %copy-start.7 = (f32[9,64]{1,0:T(8,128)S(1)}, f32[9,64]{1,0:T(8,128)}, u32[]{:S(2)}) copy-start(f32[9,64]{1,0:T(8,128)} %param.20) | copy-start | bytes 6916
  143.5 1.1 copy-start.2
where the time goes:
time: 200 us; the launch traced here: 198 us
  Pallas kernels  99.5 us (50%)
  blocking collectives  38 us (19%)
  starting transfers between devices  20.8 us (10%)
  local copies, waits for them, and re-layouts  14 us (7%)
  waiting for transfers between devices  10.1 us (5%)
  matrix products  8.92 us (4%)
  other arithmetic  6.43 us (3%)
    pallas_call x9, Pallas kernels, call(): pl.pallas_call(kernel, out_shape=shapes, grid=(steps,) if steps else (),...  91 us
    all_to_all x1, blocking collectives, local(): lax.all_to_all(result, 'chaos', split_axis=0, concat_axis=0, tiled=True)  38 us
    all_to_all x2, starting transfers between devices, exchange(): lax.all_to_all(values, axes, split_axis=0, concat_axis=0, tiled=True)  10.6 us
    broadcast_in_dim x5, local copies, waits for them, and re-layouts, local(): jnp.where(on_diag, blocks, jnp.zeros((), bf16)).reshape(pairs, LANES, LANES)  7.37 us
    dot_general x1, matrix products, dense_coupling(): jnp.einsum('ta,tb->ab', left_hot, right_hot, precision=lax.Precision.HIGH...  6.91 us
    all_to_all x1, starting transfers between devices, local(): lax.all_to_all(sent, 'chaos', split_axis=0, concat_axis=0, tiled=True)  6.46 us
    all_to_all x2, waiting for transfers between devices, exchange(): lax.all_to_all(values, axes, split_axis=0, concat_axis=0, tiled=True)  5.17 us
    all_to_all x1, waiting for transfers between devices, local(): lax.all_to_all(sent, 'chaos', split_axis=0, concat_axis=0, tiled=True)  4.93 us
  transfers between devices with their start and end apart: 4, of which 2 were waited for; matrix products, arithmetic and copies ran while one was open for 14% of the time, Pallas kernels for 36%

commit v1 on v0

v1 whole, which is shorter than its diff:
```python
import functools

import jax
import jax.numpy as jnp
import numpy as np
from jax import lax
from jax.experimental import pallas as pl
from jax.experimental.pallas import tpu as pltpu
from jax.sharding import PartitionSpec as P

ELEM_NODES = 64
LANES = 128
FACE = 16
VMEM_LIMIT = 56 * 1024 * 1024
NT = (((1,), (1,)), ((), ()))
NN = (((1,), (0,)), ((), ()))
MESH = pl.DeviceIdType.MESH


def face_nodes():
    node_rows = []
    for side_idx in range(6):
        normal_axis = side_idx // 2
        plane_level = 3 * (side_idx % 2)
        row_nodes = []
        for first_coord in range(4):
            for second_coord in range(4):
                position = [first_coord, second_coord]
                position.insert(normal_axis, plane_level)
                row_nodes.append(16 * position[0] + 4 * position[1] + position[2])
        node_rows.append(row_nodes)
    return np.array(node_rows, dtype=np.int32)


def face_select():
    table = np.zeros((LANES, 2 * LANES), np.float32)
    for side, row in enumerate(face_nodes()):
        for point, node in enumerate(row):
            for half in range(2):
                table[half * ELEM_NODES + node, half * LANES + side * FACE + point] = 1.0
    return jnp.asarray(table, jnp.bfloat16)


def mm(a, b, dims=NN):
    return lax.dot_general(a, b, dims, preferred_element_type=jnp.float32)


def iota(shape, dim):
    return lax.broadcasted_iota(jnp.int32, shape, dim)


def hot(mask):
    return jnp.where(mask, 1.0, 0.0).astype(jnp.bfloat16)


def block_diag(flat):
    spread = mm(hot(iota((LANES, 8), 0) // FACE == iota((LANES, 8), 1)), flat)
    own_row = iota((LANES, 256), 1) // FACE == iota((LANES, 256), 0) % FACE
    spread = jnp.where(own_row, spread, 0.0).astype(jnp.bfloat16)
    fold = hot(iota((256, LANES), 0) % FACE == iota((256, LANES), 1) % FACE)
    tiled = mm(spread, fold)
    same = iota((LANES, LANES), 0) // FACE == iota((LANES, LANES), 1) // FACE
    return jnp.where(same, tiled, 0.0).astype(jnp.bfloat16)


def split_rows(part):
    high = part // 16 * 16
    return high, part - high, high + 16


def swap(x):
    row, group = iota(x.shape, 1), iota(x.shape, 2) // FACE
    for k in (1, 2, 4):
        row_bit, group_bit = row // k % 2, group // k % 2
        moved = pltpu.roll(pltpu.roll(x, 8 - k, 1), FACE * k, 2)
        if k < 4:
            other = pltpu.roll(pltpu.roll(x, k, 1), LANES - FACE * k, 2)
            moved = jnp.where(row_bit < group_bit, moved, other)
        x = jnp.where(row_bit == group_bit, x, moved)
    return x


def to_rows(tiles):
    turned = [swap(t.reshape(-1, 8, LANES)) for t in tiles]
    return jnp.concatenate(
        [jnp.concatenate([t[a] for t in turned], axis=0) for a in range(turned[0].shape[0])], axis=1
    ).astype(jnp.bfloat16)


def to_tiles(rows):
    tiles = []
    for h in range(2):
        own = rows[8 * h:8 * h + 8]
        stack = jnp.stack([own[:, a * LANES:(a + 1) * LANES] for a in range(rows.shape[1] // LANES)], axis=0)
        tiles.append(swap(stack).reshape(-1, LANES))
    return tiles


def column(row):
    size = row.shape[1]
    eye = iota((size, size), 0) == iota((size, size), 1)
    return jnp.sum(jnp.where(eye, row, 0), axis=1, keepdims=True)


def split_rows(part):
    high = part // 16 * 16
    return high, part - high, high + 16


def greet(axes):
    barrier = pltpu.get_barrier_semaphore()
    for axis, count in axes:
        me = lax.axis_index(axis)
        for d in range(1, count):
            pl.semaphore_signal(barrier, 1, device_id={axis: lax.rem(me + d, count)}, device_id_type=MESH)


def meet(axes):
    pl.semaphore_wait(pltpu.get_barrier_semaphore(), sum(count - 1 for _, count in axes))


def send(src, dst, sems, d, axis, peer):
    copy = pltpu.make_async_remote_copy(
        src_ref=src, dst_ref=dst, send_sem=sems.at[0, d - 1], recv_sem=sems.at[1, d - 1],
        device_id={axis: peer}, device_id_type=MESH)
    copy.start()
    return copy


def finish(copies):
    for copy in copies:
        copy.wait()


def pack(load, store, tail_ref, part, width):
    high, low, _ = split_rows(part)
    for q in range(16):
        upper, lower = load(q)
        store(slice(q * high, (q + 1) * high), upper)
        tail_ref[q * low:(q + 1) * low, :] = lower.astype(jnp.float32)
    store(slice(16 * high, 16 * part), tail_ref[...].astype(jnp.bfloat16))


def mix(coupling_ref, block, weights):
    total = weights[0:1] * block.astype(jnp.float32)
    for k in range(coupling_ref.shape[0]):
        total = total + weights[k + 1:k + 2] * mm(coupling_ref[k], block)
    return total.astype(jnp.bfloat16)


def slot_ids(requests, n, cap, faces):
    lane = iota((1, LANES), 1)
    return lax.rem(lane // cap, n) * faces + requests


def head_kernel(
    field_ref, stiff_ref, kl_ref, triple_ref, value_ref, index_ref, die_ref, int_ref, sel_ref,
    coupling_out, out_ref, proj_out, int_out, share_out, ask_out, die_diag, int_diag,
    msg, rows, sent, wide, block_ref, faces_ref, table_ref, slots, recv, picked, fp, stiff, die_faces, tail_ref,
    share_sem, ask_sem, field_sem, slot_sem, pick_sem, *, n, ns, cap, faces,
):
    f32, bf16 = jnp.float32, jnp.bfloat16
    me_c, me_s = lax.axis_index("chaos"), lax.axis_index("space")
    axes = (("chaos", n), ("space", ns))
    greet(axes)
    part, local_nodes = field_ref.shape
    nodes = local_nodes // n
    width = nodes // 16
    per = width // LANES
    high, low, pad = split_rows(part)
    wide_lanes = pad * FACE
    modes, all_rows, _ = coupling_out.shape
    sel = sel_ref[...]

    index = index_ref[...]
    owner, seg_face = index[0:1], index[1:2]
    segs = owner.shape[1]
    r, c = iota((segs, segs), 0), iota((segs, segs), 1)
    owner_col, face_col = column(owner), column(seg_face)
    same = owner_col == owner
    rank_row = jnp.sum(jnp.where(same & (r < c), 1, 0), axis=0, keepdims=True)
    rank_col = jnp.sum(jnp.where(same & (c < r), 1, 0), axis=1, keepdims=True)
    base = me_c * (n * cap)
    lane_row = base + lax.rem(owner, n) * cap + rank_row
    lane_col = base + lax.rem(owner_col, n) * cap + rank_col
    left = hot(iota((16, segs), 0) == lax.div(owner, n))
    request = mm(left, jnp.where(c == lane_col, face_col, 0).astype(f32).astype(bf16))
    msg[...] = jnp.zeros(msg.shape, jnp.int32)
    msg[:ns, :] = request[:ns].astype(jnp.int32)
    msg[ns:ns + 1, :] = lax.div(owner, n) * LANES + lane_row
    msg[ns + 1:ns + 2, :] = index[2:3]
    meet(axes)
    share_out[me_c] = msg[...]
    copies = []
    for d in range(1, n):
        copies.append(send(msg, share_out.at[me_c], share_sem, d, "chaos", lax.rem(me_c + d, n)))

    field_copies = []
    for d in range(1, n + 1):
        peer = lax.rem(me_c + d, n)
        start = peer * nodes

        def load(q):
            cols = pl.ds(pl.multiple_of(start + q * width, LANES), width)
            return field_ref[:high, cols], field_ref[high:part, cols]

        def store(where, value):
            if d < n:
                sent[peer, where, :] = value
            else:
                wide[me_c, where, :] = value

        pack(load, store, tail_ref, part, width)
        if d < n:
            field_copies.append(send(sent.at[peer], wide.at[me_c], field_sem, d, "chaos", peer))
    finish(copies)

    total = share_out[0, :ns, :]
    for i in range(1, n):
        total = total + share_out[i, :ns, :]
    for s in range(ns):
        rows[s] = jnp.broadcast_to(total[s:s + 1, :], (8, LANES))
    ask_out[me_s] = rows[me_s]
    copies = []
    for d in range(1, ns):
        peer = lax.rem(me_s + d, ns)
        copies.append(send(rows.at[peer], ask_out.at[me_s], ask_sem, d, "space", peer))

    block_ref[...] = jnp.zeros(block_ref.shape, bf16)
    pairs = nodes // LANES
    step_pairs = block_ref.shape[0]

    def face_step(p, carry):
        for u in range(step_pairs):
            at = p * step_pairs + u
            block_ref[u, :part, :] = field_ref[:, pl.ds(pl.multiple_of(at * LANES, LANES), LANES)]
            found = mm(block_ref[u], sel)
            faces_ref[pl.ds(pl.multiple_of(at * 16, 16), 16), :] = to_rows([found[:, :LANES], found[:, LANES:]])
        return carry

    lax.fori_loop(0, n * pairs // step_pairs, face_step, 0)
    elem_rows = pairs * 16
    for i in range(n):
        code = column(share_out[i, ns + 1:ns + 2, :])
        pick = hot(iota((LANES, elem_rows), 1) == code)
        found = mm(pick[:faces], faces_ref[i * elem_rows:(i + 1) * elem_rows, :])
        table_ref[i * faces:(i + 1) * faces, :] = found.astype(bf16)
    finish(copies)

    slot_copies = []
    for d in range(1, ns + 1):
        peer = lax.rem(me_s + d, ns)
        ids = column(slot_ids(ask_out[peer, 0:1, :], n, cap, faces))
        found = mm(hot(iota((LANES, n * faces), 1) == ids), table_ref[...]).astype(bf16)
        if d < ns:
            slots[peer] = found
            slot_copies.append(send(slots.at[peer], recv.at[me_s], slot_sem, d, "space", peer))
        else:
            recv[me_s] = found

    groups = die_diag.shape[0]

    def diag_step(g, carry):
        die_diag[g] = block_diag(die_ref[g])
        int_diag[g] = block_diag(int_ref[g])
        return carry

    lax.fori_loop(0, groups, diag_step, 0)

    triples = triple_ref[...]
    value = value_ref[...]
    key, col = triples[0:1], triples[1:2]
    coarse = value.astype(bf16).astype(f32)
    at_col = iota((all_rows, key.shape[1]), 0) == col
    right = jnp.concatenate(
        [jnp.where(at_col, coarse, 0.0).astype(bf16), jnp.where(at_col, value - coarse, 0.0).astype(bf16)], axis=0
    )

    def mode_step(k, carry):
        at_row = hot(iota((all_rows, key.shape[1]), 0) + k * all_rows == key)
        both = mm(at_row, right, NT)
        coupling_out[k] = (both[:, :all_rows] + both[:, all_rows:]).astype(bf16)
        return carry

    lax.fori_loop(0, modes, mode_step, 0)

    elems = stiff_ref.shape[0]
    for t in range(ELEM_NODES // 2):
        block = stiff_ref[:, t * LANES:(t + 1) * LANES].astype(f32)
        stiff[pl.ds(2 * t, elems, stride=ELEM_NODES), :] = block
        stiff[pl.ds(2 * t + 1, elems, stride=ELEM_NODES), :] = pltpu.roll(block, ELEM_NODES, 1)

    finish(slot_copies)
    pick_copies = []
    everything = recv[...].reshape(ns * LANES, wide_lanes)
    for d in range(1, n + 1):
        peer = lax.rem(me_c + d, n)
        spot = column(share_out[peer, ns:ns + 1, :])
        found = mm(hot(iota((segs, ns * LANES), 1) == spot), everything).astype(bf16)
        if d < n:
            picked[peer] = found
            pick_copies.append(send(picked.at[peer], int_out.at[me_c], pick_sem, d, "chaos", peer))
        else:
            int_out[me_c] = found

    finish(field_copies)
    keep = iota((16, width), 0) < low
    for i in range(n):
        tail_ref[...] = wide[i, 16 * high:, :].astype(f32)
        for q in range(16):
            first = min(q * low, 16 * low - 16)
            tail = tail_ref[first:first + 16, :]
            if first < q * low:
                tail = pltpu.roll(tail, 16 - (q * low - first), 0)
            tail = jnp.where(keep, tail, 0.0).astype(bf16)
            for h in range(per):
                cols = slice(h * LANES, (h + 1) * LANES)
                fp[q * per + h, i * pad:i * pad + high, :] = wide[i, q * high:(q + 1) * high, cols]
                fp[q * per + h, i * pad + high:(i + 1) * pad, :] = tail[:, cols]

    lower = iota((ELEM_NODES, LANES), 1) < ELEM_NODES

    def element_step(p, carry):
        block = jnp.concatenate([fp[2 * p], fp[2 * p + 1]], axis=1)
        spread = jnp.where(iota((elems, 256), 1) // ELEM_NODES + 4 * p == iota((elems, 256), 0), 1.0, 0.0)
        weights = lax.dot_general(
            kl_ref[...], spread, NN, precision=lax.Precision.HIGHEST, preferred_element_type=f32)
        mixed = mix(coupling_out, block, weights)
        for h in range(2):
            at = pl.multiple_of((2 * p + h) * LANES, LANES)
            even = jnp.where(lower, stiff[pl.ds(at, ELEM_NODES), :], 0.0)
            odd = pltpu.roll(stiff[pl.ds(at + ELEM_NODES, ELEM_NODES), :], ELEM_NODES, 1)
            odd = jnp.where(lower, 0.0, odd)
            diag = jnp.concatenate([even, odd], axis=0).astype(bf16)
            out_ref[2 * p + h] = mm(mixed[:, h * LANES:(h + 1) * LANES], diag, NT)
        return carry

    lax.fori_loop(0, pairs // 2, element_step, 0)

    def die_step(p, carry):
        found = mm(fp[p], sel)
        at = pl.ds(pl.multiple_of(p * 16, 16), 16)
        for i in range(n):
            own = found[i * pad:(i + 1) * pad]
            die_faces[i, at, :] = to_rows([own[:, :LANES], own[:, LANES:]])
        return carry

    lax.fori_loop(0, pairs, die_step, 0)
    code = column(index[3:4])
    pick = hot(iota((segs, elem_rows), 1) == code)
    for i in range(n):
        found = mm(pick, die_faces[i])
        for g in range(groups // 2):
            tiles = to_tiles(found[16 * g:16 * g + 16])
            for h in range(2):
                proj_out[2 * g + h, i * pad:(i + 1) * pad, :] = tiles[h].astype(bf16)

    def project_step(g, carry):
        proj_out[g] = mm(proj_out[g], die_diag[g], NT).astype(bf16)
        return carry

    lax.fori_loop(0, groups, project_step, 0)
    finish(pick_copies)


def tail_kernel(
    faces_ref, proj_ref, die_diag, int_diag, coupling_ref, coef_ref, local_ref, index_ref, share_ref, ask_ref, sel_ref,
    returned, delta_out,
    back_send, back_recv, die_back, out_send, slots, recv, tail_ref,
    back_sem, out_sem, slot_sem, *, n, ns, cap, faces, part,
):
    f32, bf16 = jnp.float32, jnp.bfloat16
    me_c, me_s = lax.axis_index("chaos"), lax.axis_index("space")
    axes = (("chaos", n), ("space", ns))
    greet(axes)
    groups, all_rows, _ = proj_ref.shape
    pairs = local_ref.shape[0]
    high, low, pad = split_rows(part)
    wide_lanes = pad * FACE
    width = returned.shape[2]
    per = width // LANES
    segs = index_ref.shape[1]
    sel = sel_ref[...]

    def flux_step(p, carry):
        at = pl.ds(pl.multiple_of(p * 16, 16), 16)
        tiles = [to_tiles(faces_ref[i, at, :].astype(f32)) for i in range(n)]
        jumps = []
        for h in range(2):
            face = jnp.concatenate([t[h] for t in tiles], axis=0).astype(bf16)
            own = mm(face, int_diag[2 * p + h], NT)
            jumps.append((proj_ref[2 * p + h].astype(f32) - own).astype(bf16))
        spread = hot(iota((segs, 256), 1) // FACE + 16 * p == iota((segs, 256), 0))
        weights = mm(coef_ref[...], spread)
        flux = mix(coupling_ref, jnp.concatenate(jumps, axis=1), weights)
        halves = [flux[:, h * LANES:(h + 1) * LANES] for h in range(2)]
        int_side = [mm(halves[h], int_diag[2 * p + h]) for h in range(2)]
        die_side = [mm(halves[h], die_diag[2 * p + h]) for h in range(2)]
        for i in range(n):
            rows = slice(i * pad, (i + 1) * pad)
            back_send[i, at, :] = to_rows([x[rows] for x in int_side])
            die_back[i, at, :] = to_rows([x[rows] for x in die_side])
        return carry

    lax.fori_loop(0, groups // 2, flux_step, 0)
    meet(axes)
    back_copies = []
    for d in range(1, n):
        peer = lax.rem(me_c + d, n)
        back_copies.append(send(back_send.at[peer], back_recv.at[me_c], back_sem, d, "chaos", peer))
    back_recv[me_c] = back_send[me_c]

    elem_rows = pairs * 16
    place = hot(iota((elem_rows, segs), 0) == index_ref[3:4, :])
    out_copies = []
    for d in range(1, n + 1):
        peer = lax.rem(me_c + d, n)
        found = mm(place, die_back[peer])

        def load(q):
            upper, lower = [], []
            for h in range(per):
                p = q * per + h
                tiles = to_tiles(found[16 * p:16 * p + 16])
                both = jnp.concatenate(tiles, axis=1).astype(bf16)
                own = local_ref[p, pl.ds(pl.multiple_of(peer * pad, 16), pad), :] + mm(both, sel, NT)
                upper.append(own[:high])
                lower.append(own[high:part])
            return jnp.concatenate(upper, axis=1).astype(bf16), jnp.concatenate(lower, axis=1)

        def store(where, value):
            if d < n:
                out_send[peer, where, :] = value
            else:
                returned[me_c, where, :] = value

        pack(load, store, tail_ref, part, width)
        if d < n:
            out_copies.append(send(out_send.at[peer], returned.at[me_c], out_sem, d, "chaos", peer))

    finish(back_copies)
    everything = back_recv[...].reshape(n * segs, wide_lanes)
    spots = jnp.concatenate([share_ref[i, ns:ns + 1, :] for i in range(n)], axis=1)
    slot_copies = []
    for d in range(1, ns + 1):
        peer = lax.rem(me_s + d, ns)
        found = mm(hot(iota((LANES, n * segs), 0) + peer * LANES == spots), everything).astype(bf16)
        if d < ns:
            slots[peer] = found
            slot_copies.append(send(slots.at[peer], recv.at[me_s], slot_sem, d, "space", peer))
        else:
            recv[me_s] = found
    finish(slot_copies)

    ids = jnp.concatenate([slot_ids(ask_ref[s, 0:1, :], n, cap, faces) for s in range(ns)], axis=1)
    everything = recv[...].reshape(ns * LANES, wide_lanes)
    summed = mm(hot(iota((n * faces, ns * LANES), 0) == ids), everything).astype(bf16)
    for i in range(n):
        code = share_ref[i, ns + 1:ns + 2, :][:, :faces]
        found = mm(hot(iota((elem_rows, faces), 0) == code), summed[i * faces:(i + 1) * faces])
        for p in range(pairs):
            both = jnp.concatenate(to_tiles(found[16 * p:16 * p + 16]), axis=1).astype(bf16)
            delta_out[i * pairs + p] = mm(both, sel, NT)
    finish(out_copies)


def receive_kernel(in_ref, delta_ref, out_ref, tail_ref):
    part, nodes = out_ref.shape
    high, low, _ = split_rows(part)
    width = nodes // 16
    per = width // LANES
    tail_ref[...] = in_ref[0, 16 * high:, :].astype(jnp.float32)
    for q in range(16):
        for h in range(per):
            cols = slice(q * width + h * LANES, q * width + (h + 1) * LANES)
            own = slice(h * LANES, (h + 1) * LANES)
            delta = delta_ref[q * per + h]
            upper = in_ref[0, q * high:(q + 1) * high, own].astype(jnp.float32)
            out_ref[:high, cols] = (upper - delta[:high]).astype(jnp.bfloat16)
            lower = tail_ref[q * low:(q + 1) * low, own]
            out_ref[high:part, cols] = (lower - delta[high:part]).astype(jnp.bfloat16)


def call(kernel, outs, args, scratch, collective_id):
    moved = sum(x.size * x.dtype.itemsize for x in (*args, *outs))
    return pl.pallas_call(
        kernel,
        out_shape=outs,
        in_specs=[pl.BlockSpec(memory_space=pltpu.VMEM)] * len(args),
        out_specs=tuple(pl.BlockSpec(memory_space=pltpu.VMEM) for _ in outs),
        scratch_shapes=scratch,
        compiler_params=pltpu.CompilerParams(
            collective_id=collective_id, has_side_effects=True, vmem_limit_bytes=VMEM_LIMIT
        ),
        cost_estimate=pl.CostEstimate(flops=0, bytes_accessed=moved, transcendentals=0),
    )(*args)


def local(
    field,
    stiffness,
    kl_coef,
    triple_mode,
    triple_row,
    triple_col,
    triple_value,
    die_elem,
    die_side,
    seg_owner,
    seg_face,
    die_mortar,
    int_mortar,
    bump_coef,
    int_elem,
    int_side,
):
    n, ns = lax.axis_size("chaos"), lax.axis_size("space")
    part, local_nodes = field.shape
    nodes = local_nodes // n
    segs = die_elem.shape[0]
    cap = max(2, 2 * segs // (n * ns))
    faces = int_elem.shape[0]
    pairs = nodes // LANES
    modes = bump_coef.shape[1] - 1
    high, low, pad = split_rows(part)
    rows = n * pad
    lanes = pad * FACE
    groups = segs // 8
    width = nodes // 16
    bf16, f32, i32 = jnp.bfloat16, jnp.float32, jnp.int32
    sel = face_select()

    index = jnp.stack([
        seg_owner, seg_face, jnp.pad(int_elem * 8 + int_side, (0, segs - faces)), die_elem * 8 + die_side,
    ])
    triples = jnp.stack([
        triple_mode * rows + triple_row // part * pad + triple_row % part, triple_col // part * pad + triple_col % part,
    ])
    height = (ns + 2 + 7) // 8 * 8
    packed = (n, 16 * part, width)

    def sems(count):
        return pltpu.SemaphoreType.DMA((2, count - 1))

    coupling, local_out, proj, int_faces, shared, asked, die_diag, int_diag = call(
        functools.partial(head_kernel, n=n, ns=ns, cap=cap, faces=faces),
        (
            jax.ShapeDtypeStruct((modes, rows, rows), bf16),
            jax.ShapeDtypeStruct((pairs, rows, LANES), f32),
            jax.ShapeDtypeStruct((groups, rows, LANES), bf16),
            jax.ShapeDtypeStruct((n, segs, lanes), bf16),
            jax.ShapeDtypeStruct((n, height, LANES), i32),
            jax.ShapeDtypeStruct((ns, 8, LANES), i32),
            jax.ShapeDtypeStruct((groups, LANES, LANES), bf16),
            jax.ShapeDtypeStruct((groups, LANES, LANES), bf16),
        ),
        (
            field, stiffness, kl_coef, triples, triple_value.reshape(1, -1), index,
            die_mortar.reshape(groups, 8, 256), int_mortar.reshape(groups, 8, 256), sel,
        ),
        (
            pltpu.VMEM((height, LANES), i32),
            pltpu.VMEM((ns, 8, LANES), i32),
            pltpu.VMEM(packed, bf16),
            pltpu.VMEM(packed, bf16),
            pltpu.VMEM((4, pad, LANES), bf16),
            pltpu.VMEM((n * pairs * 16, lanes), bf16),
            pltpu.VMEM((n * faces, lanes), bf16),
            pltpu.VMEM((ns, LANES, lanes), bf16),
            pltpu.VMEM((ns, LANES, lanes), bf16),
            pltpu.VMEM((n, segs, lanes), bf16),
            pltpu.VMEM((pairs, rows, LANES), bf16),
            pltpu.VMEM((2 * pairs * ELEM_NODES, LANES), f32),
            pltpu.VMEM((n, pairs * 16, lanes), bf16),
            pltpu.VMEM((16 * low, width), f32),
            sems(n), sems(ns), sems(n), sems(ns), sems(n),
        ),
        0,
    )
    returned, delta = call(
        functools.partial(tail_kernel, n=n, ns=ns, cap=cap, faces=faces, part=part),
        (
            jax.ShapeDtypeStruct(packed, bf16),
            jax.ShapeDtypeStruct((n * pairs, pad, LANES), f32),
        ),
        (int_faces, proj, die_diag, int_diag, coupling, bump_coef.T, local_out, index, shared, asked, sel),
        (
            pltpu.VMEM((n, segs, lanes), bf16),
            pltpu.VMEM((n, segs, lanes), bf16),
            pltpu.VMEM((n, segs, lanes), bf16),
            pltpu.VMEM(packed, bf16),
            pltpu.VMEM((ns, LANES, lanes), bf16),
            pltpu.VMEM((ns, LANES, lanes), bf16),
            pltpu.VMEM((16 * low, width), f32),
            sems(n), sems(n), sems(ns),
        ),
        1,
    )
    return pl.pallas_call(
        receive_kernel,
        out_shape=jax.ShapeDtypeStruct((part, local_nodes), bf16),
        grid=(n,),
        in_specs=[
            pl.BlockSpec((1, 16 * part, width), lambda c: (c, 0, 0)),
            pl.BlockSpec((pairs, pad, LANES), lambda c: (c, 0, 0)),
        ],
        out_specs=pl.BlockSpec((part, nodes), lambda c: (0, c)),
        scratch_shapes=[pltpu.VMEM((16 * low, width), f32)],
    )(returned, delta)


def solution(mesh):
    in_specs = (
        P("chaos", "space"),
        P(("space", "chaos"), None),
        P(None, ("space", "chaos")),
        P(),
        P(),
        P(),
        P(),
        P(("space", "chaos")),
        P(("space", "chaos")),
        P(("space", "chaos")),
        P(("space", "chaos")),
        P(("space", "chaos"), None),
        P(("space", "chaos"), None),
        P(("space", "chaos"), None),
        P(("space", "chaos")),
        P(("space", "chaos")),
    )
    out_specs = P("chaos", "space")
    return jax.shard_map(local, mesh=mesh, in_specs=in_specs, out_specs=out_specs, check_vma=False)
```

time: 200 us -> 170 us (0.85)
  the two profiles are of different devices: /device:TPU:0 before, /device:TPU:11 now
where the time goes in v1:
time: 170 us; the launch traced here: 169 us
  Pallas kernels  163 us (96%)
  other arithmetic  4.67 us (3%)
    pallas_call x2, Pallas kernels, call(): pl.pallas_call(kernel, out_shape=outs, in_specs=[pl.BlockSpec(memory_spac...  159 us
    pallas_call x1, Pallas kernels, local(): pl.pallas_call(receive_kernel, out_shape=jax.ShapeDtypeStruct((part, loca...  4.28 us

profile of v1, /device:TPU:11, one launch (start us, length us, event | category | flops | bytes accessed | tf_op | source)
XLA Modules:
  0.0 169.2 jit_solution(6175638598190860433)
XLA Ops:
  0.0 0.7 multiply_add_fusion
  0.7 0.7 add_bitcast_fusion
  1.4 1.2 pad_add_fusion.1.index_ref
  2.6 1.3 reshape.9.value_ref
  3.9 0.7 fusion.2
  4.6 0.7 fusion.4
  5.4 0.6 pad_add_fusion.triple_ref
  6.0 84.1 %shard_map.163 = (bf16[8,192,192]{2,1,0:T(8,128)(2,1)}, f32[32,192,128]{2,1,0:T(8,128)}, bf16[16,192,128]{2,1,0:T(8,128)(2,1)}, bf16[4,128,768]{2,1,0:T(8,128)(2...) custom-call(bf16[42,16384]{1,0:T(8,128)(2,1)} %field_ref.1, ...), custom_call_target="tpu_custom_call" | custom-call | bytes 8556288 | tf_op jit(solution)/shard_map/pallas_call | solution.py:486
  90.2 74.8 %shard_map.164 = (bf16[4,672,256]{2,1,0:T(8,128)(2,1)}, f32[128,48,128]{2,1,0:T(8,128)}) custom-call(bf16[4,128,768]{2,1,0:T(8,128)(2,1)} %get-tuple-element.15.faces_ref, bf16[16,192,128]{2,1,0:T(8,128)(2,1)} %get-tuple-element.16.proj_ref, bf16[16,128,128]{2,1,0:T(8,128)(2,1)} %get-tuple-element.17.die_diag, ...), custom_call_target="tpu_custom_call" | custom-call | bytes 11014400 | tf_op jit(solution)/shard_map/pallas_call | solution.py:486
  164.9 4.3 %shard_map.165 = bf16[42,16384]{1,0:T(8,128)(2,1)} custom-call(bf16[4,672,256]{2,1,0:T(8,128)(2,1)} %get-tuple-element.23.in_ref, f32[128,48,128]{2,1,0:T(8,128)} %get-tuple-element.24.delta_ref), custom_call_target="tpu_custom_call" | custom-call | tf_op jit(solution)/shard_map/pallas_call | solution.py:599
  (2 shorter events, 0.0 us)

commit v2 on v1

--- a/solution.py
+++ b/solution.py
@@ -53,47 +53,53 @@
     return jnp.where(mask, 1.0, 0.0).astype(jnp.bfloat16)
 
 
-def block_diag(flat):
-    spread = mm(hot(iota((LANES, 8), 0) // FACE == iota((LANES, 8), 1)), flat)
-    own_row = iota((LANES, 256), 1) // FACE == iota((LANES, 256), 0) % FACE
-    spread = jnp.where(own_row, spread, 0.0).astype(jnp.bfloat16)
-    fold = hot(iota((256, LANES), 0) % FACE == iota((256, LANES), 1) % FACE)
-    tiled = mm(spread, fold)
-    same = iota((LANES, LANES), 0) // FACE == iota((LANES, LANES), 1) // FACE
-    return jnp.where(same, tiled, 0.0).astype(jnp.bfloat16)
-
-
-def split_rows(part):
-    high = part // 16 * 16
-    return high, part - high, high + 16
-
-
-def swap(x):
-    row, group = iota(x.shape, 1), iota(x.shape, 2) // FACE
+def trade(x):
+    group = iota((8, LANES), 1) // FACE
     for k in (1, 2, 4):
-        row_bit, group_bit = row // k % 2, group // k % 2
-        moved = pltpu.roll(pltpu.roll(x, 8 - k, 1), FACE * k, 2)
-        if k < 4:
-            other = pltpu.roll(pltpu.roll(x, k, 1), LANES - FACE * k, 2)
-            moved = jnp.where(row_bit < group_bit, moved, other)
-        x = jnp.where(row_bit == group_bit, x, moved)
+        upper = group // k % 2 == 1
+        y = [None] * 8
+        for v in range(8):
+            if v & k:
+                continue
+            low, high = x[v], x[v + k]
+            if high is not None:
+                y[v] = jnp.where(upper, pltpu.roll(high, FACE * k, 1), low)
+                y[v + k] = jnp.where(upper, high, pltpu.roll(low, LANES - FACE * k, 1))
+            elif low is not None:
+                y[v] = jnp.where(upper, 0.0, low)
+                y[v + k] = jnp.where(upper, 0.0, pltpu.roll(low, LANES - FACE * k, 1))
+        x = y
     return x
 
 
-def to_rows(tiles):
-    turned = [swap(t.reshape(-1, 8, LANES)) for t in tiles]
-    return jnp.concatenate(
-        [jnp.concatenate([t[a] for t in turned], axis=0) for a in range(turned[0].shape[0])], axis=1
-    ).astype(jnp.bfloat16)
-
-
-def to_tiles(rows):
-    tiles = []
-    for h in range(2):
-        own = rows[8 * h:8 * h + 8]
-        stack = jnp.stack([own[:, a * LANES:(a + 1) * LANES] for a in range(rows.shape[1] // LANES)], axis=0)
-        tiles.append(swap(stack).reshape(-1, LANES))
-    return tiles
+def to_items(turn, pad, count, store):
+    for a in range(pad // 8):
+        y = trade([turn[pl.ds(8 * a + b, 8, stride=pad), :] for b in range(8)])
+        for g in range(0, count, 2):
+            store(g, a, jnp.concatenate([y[g], y[g + 1]], axis=0).astype(jnp.bfloat16))
+
+
+def to_tiles(load, count, turn, pad):
+    for a in range(pad // 8):
+        x = []
+        for g in range(0, count, 2):
+            both = load(g, a)
+            x += [both[:8], both[8:]]
+        y = trade(x + [None] * (8 - count))
+        for b in range(8):
+            turn[pl.ds(8 * a + b, 8, stride=pad), :] = y[b]
+
+
+def face_row(elem, side):
+    return lax.div(elem, 8) * 48 + side * 8 + lax.rem(elem, 2) * 4 + lax.div(lax.rem(elem, 8), 2)
+
+
+def at_rows(start, count):
+    return pl.ds(pl.multiple_of(start, 16), count)
+
+
+def lanes_of(a):
+    return slice(a * LANES, (a + 1) * LANES)
 
 
 def column(row):
@@ -156,7 +162,7 @@
 def head_kernel(
     field_ref, stiff_ref, kl_ref, triple_ref, value_ref, index_ref, die_ref, int_ref, sel_ref,
     coupling_out, out_ref, proj_out, int_out, share_out, ask_out, die_diag, int_diag,
-    msg, rows, sent, wide, block_ref, faces_ref, table_ref, slots, recv, picked, fp, stiff, die_faces, tail_ref,
+    msg, rows, sent, wide, block_ref, faces_ref, table_ref, slots, recv, picked, fp, stiff, die_faces, items, turn, tail_ref,
     share_sem, ask_sem, field_sem, slot_sem, pick_sem, *, n, ns, cap, faces,
 ):
     f32, bf16 = jnp.float32, jnp.bfloat16
@@ -228,18 +234,26 @@
 
     block_ref[...] = jnp.zeros(block_ref.shape, bf16)
     pairs = nodes // LANES
-    step_pairs = block_ref.shape[0]
+    blocks = pairs // 4
 
     def face_step(p, carry):
-        for u in range(step_pairs):
-            at = p * step_pairs + u
-            block_ref[u, :part, :] = field_ref[:, pl.ds(pl.multiple_of(at * LANES, LANES), LANES)]
-            found = mm(block_ref[u], sel)
-            faces_ref[pl.ds(pl.multiple_of(at * 16, 16), 16), :] = to_rows([found[:, :LANES], found[:, LANES:]])
+        for w in range(2):
+            at = 2 * p + w
+            for u in range(4):
+                cols = pl.ds(pl.multiple_of((at * 4 + u) * LANES, LANES), LANES)
+                block_ref[w, u * pad:u * pad + part, :] = field_ref[:, cols]
+            found = mm(block_ref[w], sel)
+            turn[w, :4 * pad] = found[:, :LANES]
+            turn[w, 4 * pad:] = found[:, LANES:]
+
+            def store(g, a, value):
+                faces_ref[at_rows(at * 48 + g * 8, 16), lanes_of(a)] = value
+
+            to_items(turn.at[w], pad, 6, store)
         return carry
 
-    lax.fori_loop(0, n * pairs // step_pairs, face_step, 0)
-    elem_rows = pairs * 16
+    lax.fori_loop(0, n * blocks // 2, face_step, 0)
+    elem_rows = blocks * 48
     for i in range(n):
         code = column(share_out[i, ns + 1:ns + 2, :])
         pick = hot(iota((LANES, elem_rows), 1) == code)
@@ -259,13 +273,20 @@
             recv[me_s] = found
 
     groups = die_diag.shape[0]
-
-    def diag_step(g, carry):
-        die_diag[g] = block_diag(die_ref[g])
-        int_diag[g] = block_diag(int_ref[g])
-        return carry
-
-    lax.fori_loop(0, groups, diag_step, 0)
+    lane_item = iota((FACE, LANES), 1) // FACE
+    for mortar_ref, diag in ((die_ref, die_diag), (int_ref, int_diag)):
+        for blk in range(groups // 8):
+            for half in range(2):
+                y = trade([
+                    mortar_ref[blk * 64 + g // 2 * 16:blk * 64 + g // 2 * 16 + 16, lanes_of(half)].astype(f32)[
+                        g % 2 * 8:g % 2 * 8 + 8] for g in range(8)
+                ])
+                for m in range(8):
+                    turn[blk % 2, pl.ds(half * 8 + m, 8, stride=FACE), :] = y[m]
+            for t in range(8):
+                mat = turn[blk % 2, t * FACE:(t + 1) * FACE, :]
+                for g in range(8):
+                    diag[blk * 8 + t, g * FACE:(g + 1) * FACE, :] = jnp.where(lane_item == g, mat, 0.0).astype(bf16)
 
     triples = triple_ref[...]
     value = value_ref[...]
@@ -321,52 +342,60 @@
     lower = iota((ELEM_NODES, LANES), 1) < ELEM_NODES
 
     def element_step(p, carry):
-        block = jnp.concatenate([fp[2 * p], fp[2 * p + 1]], axis=1)
-        spread = jnp.where(iota((elems, 256), 1) // ELEM_NODES + 4 * p == iota((elems, 256), 0), 1.0, 0.0)
+        block = jnp.concatenate([fp[4 * p + u] for u in range(4)], axis=1)
+        spread = jnp.where(iota((elems, 512), 1) // ELEM_NODES + 8 * p == iota((elems, 512), 0), 1.0, 0.0)
         weights = lax.dot_general(
             kl_ref[...], spread, NN, precision=lax.Precision.HIGHEST, preferred_element_type=f32)
         mixed = mix(coupling_out, block, weights)
-        for h in range(2):
-            at = pl.multiple_of((2 * p + h) * LANES, LANES)
+        for h in range(4):
+            at = pl.multiple_of((4 * p + h) * LANES, LANES)
             even = jnp.where(lower, stiff[pl.ds(at, ELEM_NODES), :], 0.0)
             odd = pltpu.roll(stiff[pl.ds(at + ELEM_NODES, ELEM_NODES), :], ELEM_NODES, 1)
             odd = jnp.where(lower, 0.0, odd)
             diag = jnp.concatenate([even, odd], axis=0).astype(bf16)
-            out_ref[2 * p + h] = mm(mixed[:, h * LANES:(h + 1) * LANES], diag, NT)
+            out_ref[4 * p + h] = mm(mixed[:, lanes_of(h)], diag, NT)
         return carry
 
-    lax.fori_loop(0, pairs // 2, element_step, 0)
-
-    def die_step(p, carry):
-        found = mm(fp[p], sel)
-        at = pl.ds(pl.multiple_of(p * 16, 16), 16)
+    lax.fori_loop(0, pairs // 4, element_step, 0)
+
+    def die_step(blk, carry):
+        for u in range(4):
+            found = mm(fp[4 * blk + u], sel)
+            for i in range(n):
+                for h in range(2):
+                    turn[i, (4 * h + u) * pad:(4 * h + u + 1) * pad] = found[i * pad:(i + 1) * pad, lanes_of(h)]
         for i in range(n):
-            own = found[i * pad:(i + 1) * pad]
-            die_faces[i, at, :] = to_rows([own[:, :LANES], own[:, LANES:]])
+            def store(g, a, value):
+                die_faces[i, at_rows(blk * 48 + g * 8, 16), lanes_of(a)] = value
+
+            to_items(turn.at[i], pad, 6, store)
         return carry
 
-    lax.fori_loop(0, pairs, die_step, 0)
-    code = column(index[3:4])
-    pick = hot(iota((segs, elem_rows), 1) == code)
+    lax.fori_loop(0, blocks, die_step, 0)
+    pick = hot(iota((segs, elem_rows), 1) == column(index[3:4]))
     for i in range(n):
-        found = mm(pick, die_faces[i])
-        for g in range(groups // 2):
-            tiles = to_tiles(found[16 * g:16 * g + 16])
-            for h in range(2):
-                proj_out[2 * g + h, i * pad:(i + 1) * pad, :] = tiles[h].astype(bf16)
-
-    def project_step(g, carry):
+        items[:segs] = mm(pick, die_faces[i])
+
+        def project_step(blk, carry):
+            to_tiles(lambda g, a: items[at_rows(blk * 64 + g * 8, 16), lanes_of(a)], 8, turn.at[0], pad)
+            for t in range(8):
+                proj_out[blk * 8 + t, i * pad:(i + 1) * pad, :] = turn[0, t * pad:(t + 1) * pad].astype(bf16)
+            return carry
+
+        lax.fori_loop(0, groups // 8, project_step, 0)
+
+    def mortar_step(g, carry):
         proj_out[g] = mm(proj_out[g], die_diag[g], NT).astype(bf16)
         return carry
 
-    lax.fori_loop(0, groups, project_step, 0)
+    lax.fori_loop(0, groups, mortar_step, 0, unroll=4)
     finish(pick_copies)
 
 
 def tail_kernel(
     faces_ref, proj_ref, die_diag, int_diag, coupling_ref, coef_ref, local_ref, index_ref, share_ref, ask_ref, sel_ref,
     returned, delta_out,
-    back_send, back_recv, die_back, out_send, slots, recv, tail_ref,
+    back_send, back_recv, die_back, out_send, slots, recv, items, turn, int_turn, die_turn, stage, tail_ref,
     back_sem, out_sem, slot_sem, *, n, ns, cap, faces, part,
 ):
     f32, bf16 = jnp.float32, jnp.bfloat16
@@ -382,27 +411,42 @@
     segs = index_ref.shape[1]
     sel = sel_ref[...]
 
-    def flux_step(p, carry):
-        at = pl.ds(pl.multiple_of(p * 16, 16), 16)
-        tiles = [to_tiles(faces_ref[i, at, :].astype(f32)) for i in range(n)]
-        jumps = []
-        for h in range(2):
-            face = jnp.concatenate([t[h] for t in tiles], axis=0).astype(bf16)
-            own = mm(face, int_diag[2 * p + h], NT)
-            jumps.append((proj_ref[2 * p + h].astype(f32) - own).astype(bf16))
-        spread = hot(iota((segs, 256), 1) // FACE + 16 * p == iota((segs, 256), 0))
-        weights = mm(coef_ref[...], spread)
-        flux = mix(coupling_ref, jnp.concatenate(jumps, axis=1), weights)
-        halves = [flux[:, h * LANES:(h + 1) * LANES] for h in range(2)]
-        int_side = [mm(halves[h], int_diag[2 * p + h]) for h in range(2)]
-        die_side = [mm(halves[h], die_diag[2 * p + h]) for h in range(2)]
+    def flux_step(blk, carry):
         for i in range(n):
-            rows = slice(i * pad, (i + 1) * pad)
-            back_send[i, at, :] = to_rows([x[rows] for x in int_side])
-            die_back[i, at, :] = to_rows([x[rows] for x in die_side])
+            to_tiles(
+                lambda g, a: faces_ref[i, at_rows(blk * 64 + g * 8, 16), lanes_of(a)].astype(f32), 8, turn.at[i], pad)
+
+        for r in range(2):
+            jumps = []
+            for h in range(4):
+                t = 4 * r + h
+                face = jnp.concatenate([turn[i, t * pad:(t + 1) * pad] for i in range(n)], axis=0).astype(bf16)
+                own = mm(face, int_diag[blk * 8 + t], NT)
+                jumps.append((proj_ref[blk * 8 + t].astype(f32) - own).astype(bf16))
+            lane = iota((segs, 512), 1)
+            seg = blk * 64 + lane % LANES // FACE * 8 + 4 * r + lane // LANES
+            weights = mm(coef_ref[...], hot(seg == iota((segs, 512), 0)))
+            flux = mix(coupling_ref, jnp.concatenate(jumps, axis=1), weights)
+            for h in range(4):
+                t = 4 * r + h
+                own = flux[:, lanes_of(h)]
+                int_side = mm(own, int_diag[blk * 8 + t])
+                die_side = mm(own, die_diag[blk * 8 + t])
+                for i in range(n):
+                    int_turn[i, t * pad:(t + 1) * pad] = int_side[i * pad:(i + 1) * pad]
+                    die_turn[i, t * pad:(t + 1) * pad] = die_side[i * pad:(i + 1) * pad]
+        for i in range(n):
+            def store_int(g, a, value):
+                back_send[i, at_rows(blk * 64 + g * 8, 16), lanes_of(a)] = value
+
+            def store_die(g, a, value):
+                die_back[i, at_rows(blk * 64 + g * 8, 16), lanes_of(a)] = value
+
+            to_items(int_turn.at[i], pad, 8, store_int)
+            to_items(die_turn.at[i], pad, 8, store_die)
         return carry
 
-    lax.fori_loop(0, groups // 2, flux_step, 0)
+    lax.fori_loop(0, groups // 8, flux_step, 0)
     meet(axes)
     back_copies = []
     for d in range(1, n):
@@ -410,31 +454,36 @@
         back_copies.append(send(back_send.at[peer], back_recv.at[me_c], back_sem, d, "chaos", peer))
     back_recv[me_c] = back_send[me_c]
 
-    elem_rows = pairs * 16
+    blocks = pairs // 4
+    elem_rows = blocks * 48
     place = hot(iota((elem_rows, segs), 0) == index_ref[3:4, :])
+
+    def nodal(blk, own):
+        to_tiles(lambda g, a: items[at_rows(blk * 48 + g * 8, 16), lanes_of(a)], 6, own, pad)
+        both = jnp.concatenate([own[:4 * pad], own[4 * pad:]], axis=1).astype(bf16)
+        return mm(both, sel, NT)
+
     out_copies = []
     for d in range(1, n + 1):
         peer = lax.rem(me_c + d, n)
-        found = mm(place, die_back[peer])
-
-        def load(q):
-            upper, lower = [], []
-            for h in range(per):
-                p = q * per + h
-                tiles = to_tiles(found[16 * p:16 * p + 16])
-                both = jnp.concatenate(tiles, axis=1).astype(bf16)
-                own = local_ref[p, pl.ds(pl.multiple_of(peer * pad, 16), pad), :] + mm(both, sel, NT)
-                upper.append(own[:high])
-                lower.append(own[high:part])
-            return jnp.concatenate(upper, axis=1).astype(bf16), jnp.concatenate(lower, axis=1)
-
-        def store(where, value):
-            if d < n:
-                out_send[peer, where, :] = value
-            else:
-                returned[me_c, where, :] = value
-
-        pack(load, store, tail_ref, part, width)
+        items[...] = mm(place, die_back[peer])
+        out_block = out_send.at[peer] if d < n else returned.at[me_c]
+
+        def out_step(b, carry):
+            for w in range(2):
+                blk = 2 * b + w
+                added = nodal(blk, turn.at[w])
+                for u in range(4):
+                    own = local_ref[blk * 4 + u, at_rows(peer * pad, pad), :] + added[u * pad:(u + 1) * pad]
+                    q = (blk * 4 + u) // per
+                    out_block[at_rows(q * high, high), lanes_of(u % per)] = own[:high].astype(bf16)
+                    stage[q, :, lanes_of(u % per)] = own[high:]
+            return carry
+
+        lax.fori_loop(0, blocks // 2, out_step, 0)
+        for q in range(16):
+            tail_ref[q * low:(q + 1) * low, :] = stage[q, :low, :]
+        out_block[16 * high:, :] = tail_ref[...].astype(bf16)
         if d < n:
             out_copies.append(send(out_send.at[peer], returned.at[me_c], out_sem, d, "chaos", peer))
 
@@ -457,10 +506,17 @@
     summed = mm(hot(iota((n * faces, ns * LANES), 0) == ids), everything).astype(bf16)
     for i in range(n):
         code = share_ref[i, ns + 1:ns + 2, :][:, :faces]
-        found = mm(hot(iota((elem_rows, faces), 0) == code), summed[i * faces:(i + 1) * faces])
-        for p in range(pairs):
-            both = jnp.concatenate(to_tiles(found[16 * p:16 * p + 16]), axis=1).astype(bf16)
-            delta_out[i * pairs + p] = mm(both, sel, NT)
+        items[...] = mm(hot(iota((elem_rows, faces), 0) == code), summed[i * faces:(i + 1) * faces])
+
+        def delta_step(b, carry):
+            for w in range(2):
+                blk = 2 * b + w
+                added = nodal(blk, turn.at[w])
+                for u in range(4):
+                    delta_out[i * pairs + blk * 4 + u] = added[u * pad:(u + 1) * pad]
+            return carry
+
+        lax.fori_loop(0, blocks // 2, delta_step, 0)
     finish(out_copies)
 
 
@@ -531,7 +587,7 @@
     sel = face_select()
 
     index = jnp.stack([
-        seg_owner, seg_face, jnp.pad(int_elem * 8 + int_side, (0, segs - faces)), die_elem * 8 + die_side,
+        seg_owner, seg_face, jnp.pad(face_row(int_elem, int_side), (0, segs - faces)), face_row(die_elem, die_side),
     ])
     triples = jnp.stack([
         triple_mode * rows + triple_row // part * pad + triple_row % part, triple_col // part * pad + triple_col % part,
@@ -556,22 +612,24 @@
         ),
         (
             field, stiffness, kl_coef, triples, triple_value.reshape(1, -1), index,
-            die_mortar.reshape(groups, 8, 256), int_mortar.reshape(groups, 8, 256), sel,
+            die_mortar, int_mortar, sel,
         ),
         (
             pltpu.VMEM((height, LANES), i32),
             pltpu.VMEM((ns, 8, LANES), i32),
             pltpu.VMEM(packed, bf16),
             pltpu.VMEM(packed, bf16),
-            pltpu.VMEM((4, pad, LANES), bf16),
-            pltpu.VMEM((n * pairs * 16, lanes), bf16),
+            pltpu.VMEM((2, 4 * pad, LANES), bf16),
+            pltpu.VMEM((n * pairs * 12, lanes), bf16),
             pltpu.VMEM((n * faces, lanes), bf16),
             pltpu.VMEM((ns, LANES, lanes), bf16),
             pltpu.VMEM((ns, LANES, lanes), bf16),
             pltpu.VMEM((n, segs, lanes), bf16),
             pltpu.VMEM((pairs, rows, LANES), bf16),
             pltpu.VMEM((2 * pairs * ELEM_NODES, LANES), f32),
-            pltpu.VMEM((n, pairs * 16, lanes), bf16),
+            pltpu.VMEM((n, pairs * 12, lanes), bf16),
+            pltpu.VMEM((segs, lanes), f32),
+            pltpu.VMEM((n, 8 * pad, LANES), f32),
             pltpu.VMEM((16 * low, width), f32),
             sems(n), sems(ns), sems(n), sems(ns), sems(n),
         ),
@@ -591,6 +649,11 @@
             pltpu.VMEM(packed, bf16),
             pltpu.VMEM((ns, LANES, lanes), bf16),
             pltpu.VMEM((ns, LANES, lanes), bf16),
+            pltpu.VMEM((pairs * 12, lanes), f32),
+            pltpu.VMEM((n, 8 * pad, LANES), f32),
+            pltpu.VMEM((n, 8 * pad, LANES), f32),
+            pltpu.VMEM((n, 8 * pad, LANES), f32),
+            pltpu.VMEM((16, 16, width), f32),
             pltpu.VMEM((16 * low, width), f32),
             sems(n), sems(n), sems(ns),
         ),

time: 170 us -> 144 us (0.85)
  Pallas kernels: 163 us -> 137 us
    pallas_call x2, Pallas kernels: 159 us -> 133 us  [call(): pl.pallas_call(kernel, out_shape=outs, in_specs=[pl.BlockSpec(memory_spac...]
where the time goes in v2:
time: 144 us; the launch traced here: 143 us
  Pallas kernels  137 us (95%)
  other arithmetic  4.69 us (3%)
    pallas_call x2, Pallas kernels, call(): pl.pallas_call(kernel, out_shape=outs, in_specs=[pl.BlockSpec(memory_spac...  133 us
    pallas_call x1, Pallas kernels, local(): pl.pallas_call(receive_kernel, out_shape=jax.ShapeDtypeStruct((part, loca...  4.28 us

profile of v2, /device:TPU:11, one launch (start us, length us, event | category | flops | bytes accessed | tf_op | source)
XLA Modules:
  0.0 143.2 jit_solution(13949585672017922564)
XLA Ops:
  0.0 0.7 fusion.16
  0.7 0.7 pad_bitcast_fusion
  1.4 1.2 pad_add_fusion.1.index_ref
  2.6 1.3 reshape.3.value_ref
  3.9 0.7 fusion.2
  4.7 0.7 fusion.4
  5.4 0.6 pad_add_fusion.triple_ref
  6.0 69.6 %shard_map.171 = (bf16[8,192,192]{2,1,0:T(8,128)(2,1)}, f32[32,192,128]{2,1,0:T(8,128)}, bf16[16,192,128]{2,1,0:T(8,128)(2,1)}, bf16[4,128,768]{2,1,0:T(8,128)(2...) custom-call(bf16[42,16384]{1,0:T(8,128)(2,1)} %field_ref.1, ...), custom_call_target="tpu_custom_call" | custom-call | bytes 8556288 | tf_op jit(solution)/shard_map/pallas_call | solution.py:542
  75.7 63.3 %shard_map.172 = (bf16[4,672,256]{2,1,0:T(8,128)(2,1)}, f32[128,48,128]{2,1,0:T(8,128)}) custom-call(bf16[4,128,768]{2,1,0:T(8,128)(2,1)} %get-tuple-element.15.faces_ref, bf16[16,192,128]{2,1,0:T(8,128)(2,1)} %get-tuple-element.16.proj_ref, bf16[16,128,128]{2,1,0:T(8,128)(2,1)} %get-tuple-element.17.die_diag, ...), custom_call_target="tpu_custom_call" | custom-call | bytes 11014400 | tf_op jit(solution)/shard_map/pallas_call | solution.py:542
  139.0 4.3 %shard_map.173 = bf16[42,16384]{1,0:T(8,128)(2,1)} custom-call(bf16[4,672,256]{2,1,0:T(8,128)(2,1)} %get-tuple-element.23.in_ref, f32[128,48,128]{2,1,0:T(8,128)} %get-tuple-element.24.delta_ref), custom_call_target="tpu_custom_call" | custom-call | tf_op jit(solution)/shard_map/pallas_call | solution.py:662
  (2 shorter events, 0.0 us)

commit v3 on v2

--- a/solution.py
+++ b/solution.py
@@ -14,6 +14,7 @@
 VMEM_LIMIT = 56 * 1024 * 1024
 NT = (((1,), (1,)), ((), ()))
 NN = (((1,), (0,)), ((), ()))
+TN = (((0,), (0,)), ((), ()))
 MESH = pl.DeviceIdType.MESH
 
 
@@ -159,11 +160,18 @@
     return lax.rem(lane // cap, n) * faces + requests
 
 
-def head_kernel(
-    field_ref, stiff_ref, kl_ref, triple_ref, value_ref, index_ref, die_ref, int_ref, sel_ref,
-    coupling_out, out_ref, proj_out, int_out, share_out, ask_out, die_diag, int_diag,
+def row_of(ref):
+    return ref[...].reshape(1, -1)
+
+
+def whole_kernel(
+    field_ref, stiff_ref, kl_ref, mode_ref, row_ref, col_ref, value_ref, die_elem_ref, die_side_ref, owner_ref,
+    seg_face_ref, die_ref, int_ref, coef_ref, int_elem_ref, int_side_ref, sel_ref, back_sel_ref,
+    out_ref,
+    coupling_out, local_ref, proj_out, int_out, share_out, ask_out, die_diag, int_diag,
     msg, rows, sent, wide, block_ref, faces_ref, table_ref, slots, recv, picked, fp, stiff, die_faces, items, turn, tail_ref,
-    share_sem, ask_sem, field_sem, slot_sem, pick_sem, *, n, ns, cap, faces,
+    back_send, back_recv, die_back, out_send, returned, back_slots, back_got, int_turn, die_turn, stage, delta_ref,
+    share_sem, ask_sem, field_sem, slot_sem, pick_sem, back_sem, out_sem, back_slot_sem, *, n, ns, cap, faces,
 ):
     f32, bf16 = jnp.float32, jnp.bfloat16
     me_c, me_s = lax.axis_index("chaos"), lax.axis_index("space")
@@ -178,8 +186,8 @@
     modes, all_rows, _ = coupling_out.shape
     sel = sel_ref[...]
 
-    index = index_ref[...]
-    owner, seg_face = index[0:1], index[1:2]
+    owner, seg_face = row_of(owner_ref), row_of(seg_face_ref)
+    die_row = face_row(row_of(die_elem_ref), row_of(die_side_ref))
     segs = owner.shape[1]
     r, c = iota((segs, segs), 0), iota((segs, segs), 1)
     owner_col, face_col = column(owner), column(seg_face)
@@ -194,13 +202,7 @@
     msg[...] = jnp.zeros(msg.shape, jnp.int32)
     msg[:ns, :] = request[:ns].astype(jnp.int32)
     msg[ns:ns + 1, :] = lax.div(owner, n) * LANES + lane_row
-    msg[ns + 1:ns + 2, :] = index[2:3]
-    meet(axes)
-    share_out[me_c] = msg[...]
-    copies = []
-    for d in range(1, n):
-        copies.append(send(msg, share_out.at[me_c], share_sem, d, "chaos", lax.rem(me_c + d, n)))
-
+    msg[ns + 1:ns + 2, :faces] = face_row(row_of(int_elem_ref), row_of(int_side_ref))
     field_copies = []
     for d in range(1, n + 1):
         peer = lax.rem(me_c + d, n)
@@ -217,6 +219,12 @@
                 wide[me_c, where, :] = value
 
         pack(load, store, tail_ref, part, width)
+        if d == 1:
+            meet(axes)
+            share_out[me_c] = msg[...]
+            copies = [
+                send(msg, share_out.at[me_c], share_sem, e, "chaos", lax.rem(me_c + e, n)) for e in range(1, n)
+            ]
         if d < n:
             field_copies.append(send(sent.at[peer], wide.at[me_c], field_sem, d, "chaos", peer))
     finish(copies)
@@ -237,8 +245,8 @@
     blocks = pairs // 4
 
     def face_step(p, carry):
-        for w in range(2):
-            at = 2 * p + w
+        for w in range(4):
+            at = 4 * p + w
             for u in range(4):
                 cols = pl.ds(pl.multiple_of((at * 4 + u) * LANES, LANES), LANES)
                 block_ref[w, u * pad:u * pad + part, :] = field_ref[:, cols]
@@ -252,7 +260,7 @@
             to_items(turn.at[w], pad, 6, store)
         return carry
 
-    lax.fori_loop(0, n * blocks // 2, face_step, 0)
+    lax.fori_loop(0, n * blocks // 4, face_step, 0)
     elem_rows = blocks * 48
     for i in range(n):
         code = column(share_out[i, ns + 1:ns + 2, :])
@@ -288,9 +296,12 @@
                 for g in range(8):
                     diag[blk * 8 + t, g * FACE:(g + 1) * FACE, :] = jnp.where(lane_item == g, mat, 0.0).astype(bf16)
 
-    triples = triple_ref[...]
-    value = value_ref[...]
-    key, col = triples[0:1], triples[1:2]
+    def padded(chaos):
+        return chaos + sum(jnp.where(chaos >= i * part, pad - part, 0) for i in range(1, n))
+
+    value = row_of(value_ref)
+    key = row_of(mode_ref) * all_rows + padded(row_of(row_ref))
+    col = padded(row_of(col_ref))
     coarse = value.astype(bf16).astype(f32)
     at_col = iota((all_rows, key.shape[1]), 0) == col
     right = jnp.concatenate(
@@ -353,7 +364,7 @@
             odd = pltpu.roll(stiff[pl.ds(at + ELEM_NODES, ELEM_NODES), :], ELEM_NODES, 1)
             odd = jnp.where(lower, 0.0, odd)
             diag = jnp.concatenate([even, odd], axis=0).astype(bf16)
-            out_ref[4 * p + h] = mm(mixed[:, lanes_of(h)], diag, NT)
+            local_ref[4 * p + h] = mm(mixed[:, lanes_of(h)], diag, NT)
         return carry
 
     lax.fori_loop(0, pairs // 4, element_step, 0)
@@ -372,7 +383,7 @@
         return carry
 
     lax.fori_loop(0, blocks, die_step, 0)
-    pick = hot(iota((segs, elem_rows), 1) == column(index[3:4]))
+    pick = hot(iota((segs, elem_rows), 1) == column(die_row))
     for i in range(n):
         items[:segs] = mm(pick, die_faces[i])
 
@@ -390,31 +401,12 @@
 
     lax.fori_loop(0, groups, mortar_step, 0, unroll=4)
     finish(pick_copies)
-
-
-def tail_kernel(
-    faces_ref, proj_ref, die_diag, int_diag, coupling_ref, coef_ref, local_ref, index_ref, share_ref, ask_ref, sel_ref,
-    returned, delta_out,
-    back_send, back_recv, die_back, out_send, slots, recv, items, turn, int_turn, die_turn, stage, tail_ref,
-    back_sem, out_sem, slot_sem, *, n, ns, cap, faces, part,
-):
-    f32, bf16 = jnp.float32, jnp.bfloat16
-    me_c, me_s = lax.axis_index("chaos"), lax.axis_index("space")
-    axes = (("chaos", n), ("space", ns))
-    greet(axes)
-    groups, all_rows, _ = proj_ref.shape
-    pairs = local_ref.shape[0]
-    high, low, pad = split_rows(part)
-    wide_lanes = pad * FACE
-    width = returned.shape[2]
-    per = width // LANES
-    segs = index_ref.shape[1]
-    sel = sel_ref[...]
+    back_sel = back_sel_ref[...]
 
     def flux_step(blk, carry):
         for i in range(n):
             to_tiles(
-                lambda g, a: faces_ref[i, at_rows(blk * 64 + g * 8, 16), lanes_of(a)].astype(f32), 8, turn.at[i], pad)
+                lambda g, a: int_out[i, at_rows(blk * 64 + g * 8, 16), lanes_of(a)].astype(f32), 8, turn.at[i], pad)
 
         for r in range(2):
             jumps = []
@@ -422,11 +414,12 @@
                 t = 4 * r + h
                 face = jnp.concatenate([turn[i, t * pad:(t + 1) * pad] for i in range(n)], axis=0).astype(bf16)
                 own = mm(face, int_diag[blk * 8 + t], NT)
-                jumps.append((proj_ref[blk * 8 + t].astype(f32) - own).astype(bf16))
+                jumps.append((proj_out[blk * 8 + t].astype(f32) - own).astype(bf16))
             lane = iota((segs, 512), 1)
             seg = blk * 64 + lane % LANES // FACE * 8 + 4 * r + lane // LANES
-            weights = mm(coef_ref[...], hot(seg == iota((segs, 512), 0)))
-            flux = mix(coupling_ref, jnp.concatenate(jumps, axis=1), weights)
+            weights = lax.dot_general(
+                coef_ref[...], hot(seg == iota((segs, 512), 0)), TN, preferred_element_type=f32)
+            flux = mix(coupling_out, jnp.concatenate(jumps, axis=1), weights)
             for h in range(4):
                 t = 4 * r + h
                 own = flux[:, lanes_of(h)]
@@ -447,21 +440,18 @@
         return carry
 
     lax.fori_loop(0, groups // 8, flux_step, 0)
-    meet(axes)
     back_copies = []
     for d in range(1, n):
         peer = lax.rem(me_c + d, n)
         back_copies.append(send(back_send.at[peer], back_recv.at[me_c], back_sem, d, "chaos", peer))
     back_recv[me_c] = back_send[me_c]
 
-    blocks = pairs // 4
-    elem_rows = blocks * 48
-    place = hot(iota((elem_rows, segs), 0) == index_ref[3:4, :])
+    place = hot(iota((elem_rows, segs), 0) == die_row)
 
     def nodal(blk, own):
         to_tiles(lambda g, a: items[at_rows(blk * 48 + g * 8, 16), lanes_of(a)], 6, own, pad)
         both = jnp.concatenate([own[:4 * pad], own[4 * pad:]], axis=1).astype(bf16)
-        return mm(both, sel, NT)
+        return mm(both, back_sel)
 
     out_copies = []
     for d in range(1, n + 1):
@@ -470,8 +460,8 @@
         out_block = out_send.at[peer] if d < n else returned.at[me_c]
 
         def out_step(b, carry):
-            for w in range(2):
-                blk = 2 * b + w
+            for w in range(4):
+                blk = 4 * b + w
                 added = nodal(blk, turn.at[w])
                 for u in range(4):
                     own = local_ref[blk * 4 + u, at_rows(peer * pad, pad), :] + added[u * pad:(u + 1) * pad]
@@ -480,76 +470,59 @@
                     stage[q, :, lanes_of(u % per)] = own[high:]
             return carry
 
-        lax.fori_loop(0, blocks // 2, out_step, 0)
+        lax.fori_loop(0, blocks // 4, out_step, 0)
         for q in range(16):
             tail_ref[q * low:(q + 1) * low, :] = stage[q, :low, :]
         out_block[16 * high:, :] = tail_ref[...].astype(bf16)
-        if d < n:
-            out_copies.append(send(out_send.at[peer], returned.at[me_c], out_sem, d, "chaos", peer))
 
     finish(back_copies)
+    for d in range(1, n):
+        peer = lax.rem(me_c + d, n)
+        out_copies.append(send(out_send.at[peer], returned.at[me_c], out_sem, d, "chaos", peer))
     everything = back_recv[...].reshape(n * segs, wide_lanes)
-    spots = jnp.concatenate([share_ref[i, ns:ns + 1, :] for i in range(n)], axis=1)
+    spots = jnp.concatenate([share_out[i, ns:ns + 1, :] for i in range(n)], axis=1)
     slot_copies = []
     for d in range(1, ns + 1):
         peer = lax.rem(me_s + d, ns)
         found = mm(hot(iota((LANES, n * segs), 0) + peer * LANES == spots), everything).astype(bf16)
         if d < ns:
-            slots[peer] = found
-            slot_copies.append(send(slots.at[peer], recv.at[me_s], slot_sem, d, "space", peer))
+            back_slots[peer] = found
+            slot_copies.append(send(back_slots.at[peer], back_got.at[me_s], back_slot_sem, d, "space", peer))
         else:
-            recv[me_s] = found
+            back_got[me_s] = found
     finish(slot_copies)
 
-    ids = jnp.concatenate([slot_ids(ask_ref[s, 0:1, :], n, cap, faces) for s in range(ns)], axis=1)
-    everything = recv[...].reshape(ns * LANES, wide_lanes)
+    ids = jnp.concatenate([slot_ids(ask_out[s, 0:1, :], n, cap, faces) for s in range(ns)], axis=1)
+    everything = back_got[...].reshape(ns * LANES, wide_lanes)
     summed = mm(hot(iota((n * faces, ns * LANES), 0) == ids), everything).astype(bf16)
     for i in range(n):
-        code = share_ref[i, ns + 1:ns + 2, :][:, :faces]
+        code = share_out[i, ns + 1:ns + 2, :][:, :faces]
         items[...] = mm(hot(iota((elem_rows, faces), 0) == code), summed[i * faces:(i + 1) * faces])
 
         def delta_step(b, carry):
-            for w in range(2):
-                blk = 2 * b + w
+            for w in range(4):
+                blk = 4 * b + w
                 added = nodal(blk, turn.at[w])
                 for u in range(4):
-                    delta_out[i * pairs + blk * 4 + u] = added[u * pad:(u + 1) * pad]
+                    delta_ref[i * pairs + blk * 4 + u] = added[u * pad:(u + 1) * pad]
             return carry
 
-        lax.fori_loop(0, blocks // 2, delta_step, 0)
-    finish(out_copies)
-
-
-def receive_kernel(in_ref, delta_ref, out_ref, tail_ref):
-    part, nodes = out_ref.shape
-    high, low, _ = split_rows(part)
-    width = nodes // 16
-    per = width // LANES
-    tail_ref[...] = in_ref[0, 16 * high:, :].astype(jnp.float32)
-    for q in range(16):
-        for h in range(per):
-            cols = slice(q * width + h * LANES, q * width + (h + 1) * LANES)
-            own = slice(h * LANES, (h + 1) * LANES)
-            delta = delta_ref[q * per + h]
-            upper = in_ref[0, q * high:(q + 1) * high, own].astype(jnp.float32)
-            out_ref[:high, cols] = (upper - delta[:high]).astype(jnp.bfloat16)
-            lower = tail_ref[q * low:(q + 1) * low, own]
-            out_ref[high:part, cols] = (lower - delta[high:part]).astype(jnp.bfloat16)
-
-
-def call(kernel, outs, args, scratch, collective_id):
-    moved = sum(x.size * x.dtype.itemsize for x in (*args, *outs))
-    return pl.pallas_call(
-        kernel,
-        out_shape=outs,
-        in_specs=[pl.BlockSpec(memory_space=pltpu.VMEM)] * len(args),
-        out_specs=tuple(pl.BlockSpec(memory_space=pltpu.VMEM) for _ in outs),
-        scratch_shapes=scratch,
-        compiler_params=pltpu.CompilerParams(
-            collective_id=collective_id, has_side_effects=True, vmem_limit_bytes=VMEM_LIMIT
-        ),
-        cost_estimate=pl.CostEstimate(flops=0, bytes_accessed=moved, transcendentals=0),
-    )(*args)
+        lax.fori_loop(0, blocks // 4, delta_step, 0)
+    def place_out(block):
+        tail_ref[...] = returned[block, 16 * high:, :].astype(f32)
+        for q in range(16):
+            for h in range(per):
+                cols = pl.ds(pl.multiple_of(block * nodes + (q * per + h) * LANES, LANES), LANES)
+                delta = delta_ref[block * pairs + q * per + h]
+                upper = returned[block, q * high:(q + 1) * high, lanes_of(h)].astype(f32)
+                out_ref[:high, cols] = (upper - delta[:high]).astype(bf16)
+                lower = tail_ref[q * low:(q + 1) * low, lanes_of(h)]
+                out_ref[high:part, cols] = (lower - delta[high:part]).astype(bf16)
+
+    place_out(me_c)
+    for d, copy in enumerate(out_copies, 1):
+        copy.wait()
+        place_out(lax.rem(me_c + n - d, n))
 
 
 def local(
@@ -586,40 +559,31 @@
     bf16, f32, i32 = jnp.bfloat16, jnp.float32, jnp.int32
     sel = face_select()
 
-    index = jnp.stack([
-        seg_owner, seg_face, jnp.pad(face_row(int_elem, int_side), (0, segs - faces)), face_row(die_elem, die_side),
-    ])
-    triples = jnp.stack([
-        triple_mode * rows + triple_row // part * pad + triple_row % part, triple_col // part * pad + triple_col % part,
-    ])
     height = (ns + 2 + 7) // 8 * 8
     packed = (n, 16 * part, width)
 
     def sems(count):
         return pltpu.SemaphoreType.DMA((2, count - 1))
 
-    coupling, local_out, proj, int_faces, shared, asked, die_diag, int_diag = call(
-        functools.partial(head_kernel, n=n, ns=ns, cap=cap, faces=faces),
-        (
-            jax.ShapeDtypeStruct((modes, rows, rows), bf16),
-            jax.ShapeDtypeStruct((pairs, rows, LANES), f32),
-            jax.ShapeDtypeStruct((groups, rows, LANES), bf16),
-            jax.ShapeDtypeStruct((n, segs, lanes), bf16),
-            jax.ShapeDtypeStruct((n, height, LANES), i32),
-            jax.ShapeDtypeStruct((ns, 8, LANES), i32),
-            jax.ShapeDtypeStruct((groups, LANES, LANES), bf16),
-            jax.ShapeDtypeStruct((groups, LANES, LANES), bf16),
-        ),
-        (
-            field, stiffness, kl_coef, triples, triple_value.reshape(1, -1), index,
-            die_mortar, int_mortar, sel,
-        ),
-        (
+    return pl.pallas_call(
+        functools.partial(whole_kernel, n=n, ns=ns, cap=cap, faces=faces),
+        out_shape=jax.ShapeDtypeStruct((part, local_nodes), bf16),
+        in_specs=[pl.BlockSpec(memory_space=pltpu.VMEM)] * 18,
+        out_specs=pl.BlockSpec(memory_space=pltpu.VMEM),
+        scratch_shapes=(
+            pltpu.VMEM((modes, rows, rows), bf16),
+            pltpu.VMEM((pairs, rows, LANES), f32),
+            pltpu.VMEM((groups, rows, LANES), bf16),
+            pltpu.VMEM((n, segs, lanes), bf16),
+            pltpu.VMEM((n, height, LANES), i32),
+            pltpu.VMEM((ns, 8, LANES), i32),
+            pltpu.VMEM((groups, LANES, LANES), bf16),
+            pltpu.VMEM((groups, LANES, LANES), bf16),
             pltpu.VMEM((height, LANES), i32),
             pltpu.VMEM((ns, 8, LANES), i32),
             pltpu.VMEM(packed, bf16),
             pltpu.VMEM(packed, bf16),
-            pltpu.VMEM((2, 4 * pad, LANES), bf16),
+            pltpu.VMEM((4, 4 * pad, LANES), bf16),
             pltpu.VMEM((n * pairs * 12, lanes), bf16),
             pltpu.VMEM((n * faces, lanes), bf16),
             pltpu.VMEM((ns, LANES, lanes), bf16),
@@ -628,48 +592,28 @@
             pltpu.VMEM((pairs, rows, LANES), bf16),
             pltpu.VMEM((2 * pairs * ELEM_NODES, LANES), f32),
             pltpu.VMEM((n, pairs * 12, lanes), bf16),
-            pltpu.VMEM((segs, lanes), f32),
-            pltpu.VMEM((n, 8 * pad, LANES), f32),
+            pltpu.VMEM((pairs * 12, lanes), f32),
+            pltpu.VMEM((max(n, 4), 8 * pad, LANES), f32),
             pltpu.VMEM((16 * low, width), f32),
-            sems(n), sems(ns), sems(n), sems(ns), sems(n),
-        ),
-        0,
-    )
-    returned, delta = call(
-        functools.partial(tail_kernel, n=n, ns=ns, cap=cap, faces=faces, part=part),
-        (
-            jax.ShapeDtypeStruct(packed, bf16),
-            jax.ShapeDtypeStruct((n * pairs, pad, LANES), f32),
-        ),
-        (int_faces, proj, die_diag, int_diag, coupling, bump_coef.T, local_out, index, shared, asked, sel),
-        (
             pltpu.VMEM((n, segs, lanes), bf16),
             pltpu.VMEM((n, segs, lanes), bf16),
             pltpu.VMEM((n, segs, lanes), bf16),
             pltpu.VMEM(packed, bf16),
+            pltpu.VMEM(packed, bf16),
             pltpu.VMEM((ns, LANES, lanes), bf16),
             pltpu.VMEM((ns, LANES, lanes), bf16),
-            pltpu.VMEM((pairs * 12, lanes), f32),
-            pltpu.VMEM((n, 8 * pad, LANES), f32),
             pltpu.VMEM((n, 8 * pad, LANES), f32),
             pltpu.VMEM((n, 8 * pad, LANES), f32),
             pltpu.VMEM((16, 16, width), f32),
-            pltpu.VMEM((16 * low, width), f32),
-            sems(n), sems(n), sems(ns),
+            pltpu.VMEM((n * pairs, pad, LANES), f32),
+            sems(n), sems(ns), sems(n), sems(ns), sems(n), sems(n), sems(n), sems(ns),
         ),
-        1,
+        compiler_params=pltpu.CompilerParams(collective_id=0, has_side_effects=True, vmem_limit_bytes=VMEM_LIMIT),
+        cost_estimate=pl.CostEstimate(flops=4 * modes * rows * rows * nodes, bytes_accessed=8 << 20, transcendentals=0),
+    )(
+        field, stiffness, kl_coef, triple_mode, triple_row, triple_col, triple_value, die_elem, die_side, seg_owner,
+        seg_face, die_mortar, int_mortar, bump_coef, int_elem, int_side, sel, sel.T,
     )
-    return pl.pallas_call(
-        receive_kernel,
-        out_shape=jax.ShapeDtypeStruct((part, local_nodes), bf16),
-        grid=(n,),
-        in_specs=[
-            pl.BlockSpec((1, 16 * part, width), lambda c: (c, 0, 0)),
-            pl.BlockSpec((pairs, pad, LANES), lambda c: (c, 0, 0)),
-        ],
-        out_specs=pl.BlockSpec((part, nodes), lambda c: (0, c)),
-        scratch_shapes=[pltpu.VMEM((16 * low, width), f32)],
-    )(returned, delta)
 
 
 def solution(mesh):

time: 144 us -> 127 us (0.88)
  Pallas kernels: 137 us -> 122 us
  other arithmetic: 4.69 us -> 0 us
  local copies, waits for them, and re-layouts: 1.33 us -> 4.06 us
    pallas_call x3 -> x1, Pallas kernels: 137 us -> 122 us  [local(): pl.pallas_call(functools.partial(whole_kernel, n=n, ns=ns, cap=cap, faces...]
    unnamed x0 -> x2, local copies, waits for them, and re-layouts: none -> 4.06 us
    another operation x3 -> x0, other arithmetic: 2.53 us -> none  [the longest x2 1.9 us: local(): jnp.stack([seg_owner, seg_face, jnp.pad(face_row(int_elem, int_side), (0,...]
    add x3 -> x0, other arithmetic: 2.16 us -> none  [the longest x1 0.74 us: local(): triple_mode * rows + triple_row // part * pad + triple_row % part]
where the time goes in v3:
time: 127 us; the launch traced here: 126 us
  Pallas kernels  122 us (96%)
  local copies, waits for them, and re-layouts  4.06 us (3%)
    pallas_call x1, Pallas kernels, local(): pl.pallas_call(functools.partial(whole_kernel, n=n, ns=ns, cap=cap, faces...  122 us
    unnamed x2, local copies, waits for them, and re-layouts  4.06 us

profile of v3, /device:TPU:11, one launch (start us, length us, event | category | flops | bytes accessed | tf_op | source)
XLA Modules:
  0.0 126.2 jit_solution(15054419109211352994)
XLA Ops:
  0.0 1.4 %copy.18.coef_ref = bf16[128,9]{1,0:T(8,128)(2,1)} copy(bf16[128,9]{0,1:T(8,128)(2,1)} %param.30) | data formatting | bytes 4608 | tf_op args[13]
  1.4 122.1 %shard_map.163 = bf16[42,16384]{1,0:T(8,128)(2,1)} custom-call(bf16[42,16384]{1,0:T(8,128)(2,1)} %field_ref.1, bf16[64,4096]{1,0:T(8,128)(2,1)} %stiff_ref.1, f32[9,64]{1,0:T(8,128)} %kl_ref.1, s32[2688]{0:T(1024)} %mode_ref.1, s32[2688]{0:T(1024)} %row_ref.1, s32[2688]{0:T(1024)} %col_ref.1, f32[2688]{0:T(1024)} %value_ref.1, s32[128]{0:T(128)} %die_elem_ref.1, ...), custom_call_target="tpu_custom_call" | custom-call | flops 4831838208 | bytes 8388608 | tf_op jit(solution)/shard_map/pallas_call | solution.py:568
  123.5 2.7 %copy.20 = bf16[42,16384]{1,0:T(8,128)(2,1)} copy(bf16[42,16384]{1,0:T(8,128)(2,1)} %shard_map.163) | data formatting | bytes 2752512

commit v4 on v3

--- a/solution.py
+++ b/solution.py
@@ -14,7 +14,6 @@
 VMEM_LIMIT = 56 * 1024 * 1024
 NT = (((1,), (1,)), ((), ()))
 NN = (((1,), (0,)), ((), ()))
-TN = (((0,), (0,)), ((), ()))
 MESH = pl.DeviceIdType.MESH
 
 
@@ -96,7 +95,7 @@
 
 
 def at_rows(start, count):
-    return pl.ds(pl.multiple_of(start, 16), count)
+    return pl.ds(start if isinstance(start, int) else pl.multiple_of(start, 16), count)
 
 
 def lanes_of(a):
@@ -126,10 +125,14 @@
     pl.semaphore_wait(pltpu.get_barrier_semaphore(), sum(count - 1 for _, count in axes))
 
 
-def send(src, dst, sems, d, axis, peer):
-    copy = pltpu.make_async_remote_copy(
+def describe(src, dst, sems, d, axis, peer):
+    return pltpu.make_async_remote_copy(
         src_ref=src, dst_ref=dst, send_sem=sems.at[0, d - 1], recv_sem=sems.at[1, d - 1],
         device_id={axis: peer}, device_id_type=MESH)
+
+
+def send(*args):
+    copy = describe(*args)
     copy.start()
     return copy
 
@@ -367,15 +370,15 @@
             local_ref[4 * p + h] = mm(mixed[:, lanes_of(h)], diag, NT)
         return carry
 
-    lax.fori_loop(0, pairs // 4, element_step, 0)
-
     def die_step(blk, carry):
         for u in range(4):
             found = mm(fp[4 * blk + u], sel)
             for i in range(n):
                 for h in range(2):
                     turn[i, (4 * h + u) * pad:(4 * h + u + 1) * pad] = found[i * pad:(i + 1) * pad, lanes_of(h)]
-        for i in range(n):
+        for d in range(1, n):
+            i = lax.rem(me_c + d, n)
+
             def store(g, a, value):
                 die_faces[i, at_rows(blk * 48 + g * 8, 16), lanes_of(a)] = value
 
@@ -383,6 +386,7 @@
         return carry
 
     lax.fori_loop(0, blocks, die_step, 0)
+    die_faces[me_c] = faces_ref[at_rows(me_c * elem_rows, elem_rows), :]
     pick = hot(iota((segs, elem_rows), 1) == column(die_row))
     for i in range(n):
         items[:segs] = mm(pick, die_faces[i])
@@ -400,8 +404,13 @@
         return carry
 
     lax.fori_loop(0, groups, mortar_step, 0, unroll=4)
+    lax.fori_loop(0, pairs // 8, element_step, 0)
     finish(pick_copies)
     back_sel = back_sel_ref[...]
+
+    def back_part(blk, d):
+        own, peer = at_rows(blk * 64, 64), lax.rem(me_c + d, n)
+        return back_send.at[peer, own], back_recv.at[me_c, own], back_sem, d + blk * (n - 1), "chaos", peer
 
     def flux_step(blk, carry):
         for i in range(n):
@@ -417,8 +426,7 @@
                 jumps.append((proj_out[blk * 8 + t].astype(f32) - own).astype(bf16))
             lane = iota((segs, 512), 1)
             seg = blk * 64 + lane % LANES // FACE * 8 + 4 * r + lane // LANES
-            weights = lax.dot_general(
-                coef_ref[...], hot(seg == iota((segs, 512), 0)), TN, preferred_element_type=f32)
+            weights = mm(coef_ref[...], hot(seg == iota((segs, 512), 0)))
             flux = mix(coupling_out, jnp.concatenate(jumps, axis=1), weights)
             for h in range(4):
                 t = 4 * r + h
@@ -437,20 +445,20 @@
 
             to_items(int_turn.at[i], pad, 8, store_int)
             to_items(die_turn.at[i], pad, 8, store_die)
+        for d in range(1, n):
+            send(*back_part(blk, d))
         return carry
 
     lax.fori_loop(0, groups // 8, flux_step, 0)
-    back_copies = []
-    for d in range(1, n):
-        peer = lax.rem(me_c + d, n)
-        back_copies.append(send(back_send.at[peer], back_recv.at[me_c], back_sem, d, "chaos", peer))
+    back_copies = [describe(*back_part(blk, d)) for blk in range(groups // 8) for d in range(1, n)]
     back_recv[me_c] = back_send[me_c]
+    lax.fori_loop(pairs // 8, pairs // 4, element_step, 0)
 
     place = hot(iota((elem_rows, segs), 0) == die_row)
 
-    def nodal(blk, own):
-        to_tiles(lambda g, a: items[at_rows(blk * 48 + g * 8, 16), lanes_of(a)], 6, own, pad)
-        both = jnp.concatenate([own[:4 * pad], own[4 * pad:]], axis=1).astype(bf16)
+    def nodal(blk, own, size):
+        to_tiles(lambda g, a: items[at_rows(blk * 48 + g * 8, 16), lanes_of(a)], 6, own, size)
+        both = jnp.concatenate([own[:4 * size], own[4 * size:8 * size]], axis=1).astype(bf16)
         return mm(both, back_sel)
 
     out_copies = []
@@ -462,7 +470,7 @@
         def out_step(b, carry):
             for w in range(4):
                 blk = 4 * b + w
-                added = nodal(blk, turn.at[w])
+                added = nodal(blk, turn.at[w], pad)
                 for u in range(4):
                     own = local_ref[blk * 4 + u, at_rows(peer * pad, pad), :] + added[u * pad:(u + 1) * pad]
                     q = (blk * 4 + u) // per
@@ -481,33 +489,55 @@
         out_copies.append(send(out_send.at[peer], returned.at[me_c], out_sem, d, "chaos", peer))
     everything = back_recv[...].reshape(n * segs, wide_lanes)
     spots = jnp.concatenate([share_out[i, ns:ns + 1, :] for i in range(n)], axis=1)
-    slot_copies = []
-    for d in range(1, ns + 1):
-        peer = lax.rem(me_s + d, ns)
-        found = mm(hot(iota((LANES, n * segs), 0) + peer * LANES == spots), everything).astype(bf16)
-        if d < ns:
-            back_slots[peer] = found
-            slot_copies.append(send(back_slots.at[peer], back_got.at[me_s], back_slot_sem, d, "space", peer))
-        else:
-            back_got[me_s] = found
-    finish(slot_copies)
+    size, half_lanes = pad, wide_lanes
+
+    def fill(half):
+        for d in range(1, ns + 1):
+            peer = lax.rem(me_s + d, ns)
+            place = hot(iota((LANES, n * segs), 0) + peer * LANES == spots)
+            found = mm(place, everything[:, half * half_lanes:(half + 1) * half_lanes]).astype(bf16)
+            if d < ns:
+                back_slots[half, peer] = found
+                if half == 0:
+                    start(half, d, peer)
+            else:
+                back_got[half, me_s] = found
+
+    half_copies = [[], []]
+
+    def start(half, d, peer):
+        half_copies[half].append(send(
+            back_slots.at[half, peer], back_got.at[half, me_s], back_slot_sem, d + half * (ns - 1), "space", peer))
 
     ids = jnp.concatenate([slot_ids(ask_out[s, 0:1, :], n, cap, faces) for s in range(ns)], axis=1)
-    everything = back_got[...].reshape(ns * LANES, wide_lanes)
-    summed = mm(hot(iota((n * faces, ns * LANES), 0) == ids), everything).astype(bf16)
-    for i in range(n):
-        code = share_out[i, ns + 1:ns + 2, :][:, :faces]
-        items[...] = mm(hot(iota((elem_rows, faces), 0) == code), summed[i * faces:(i + 1) * faces])
-
-        def delta_step(b, carry):
-            for w in range(4):
-                blk = 4 * b + w
-                added = nodal(blk, turn.at[w])
-                for u in range(4):
-                    delta_ref[i * pairs + blk * 4 + u] = added[u * pad:(u + 1) * pad]
+
+    def gather(half):
+        got = back_got[half].reshape(ns * LANES, half_lanes)
+        table_ref[:, :half_lanes] = mm(hot(iota((n * faces, ns * LANES), 0) == ids), got).astype(bf16)
+
+        def gather_step(i, carry):
+            code = share_out[i, ns + 1:ns + 2, :][:, :faces]
+            items[:, :half_lanes] = mm(
+                hot(iota((elem_rows, faces), 0) == code), table_ref[at_rows(i * faces, faces), :half_lanes])
+
+            def delta_step(b, carry):
+                for w in range(4):
+                    blk = 4 * b + w
+                    added = nodal(blk, turn.at[w], size)
+                    for u in range(4):
+                        delta_ref[i * pairs + blk * 4 + u, half * size:(half + 1) * size] = (
+                            added[u * size:(u + 1) * size])
+                return carry
+
+            lax.fori_loop(0, blocks // 4, delta_step, 0)
             return carry
 
-        lax.fori_loop(0, blocks // 4, delta_step, 0)
+        lax.fori_loop(0, n, gather_step, 0)
+
+    fill(0)
+    finish(half_copies[0])
+    gather(0)
+
     def place_out(block):
         tail_ref[...] = returned[block, 16 * high:, :].astype(f32)
         for q in range(16):
@@ -562,8 +592,8 @@
     height = (ns + 2 + 7) // 8 * 8
     packed = (n, 16 * part, width)
 
-    def sems(count):
-        return pltpu.SemaphoreType.DMA((2, count - 1))
+    def sems(count, rounds=1):
+        return pltpu.SemaphoreType.DMA((2, rounds * (count - 1)))
 
     return pl.pallas_call(
         functools.partial(whole_kernel, n=n, ns=ns, cap=cap, faces=faces),
@@ -600,19 +630,19 @@
             pltpu.VMEM((n, segs, lanes), bf16),
             pltpu.VMEM(packed, bf16),
             pltpu.VMEM(packed, bf16),
-            pltpu.VMEM((ns, LANES, lanes), bf16),
-            pltpu.VMEM((ns, LANES, lanes), bf16),
+            pltpu.VMEM((1, ns, LANES, lanes), bf16),
+            pltpu.VMEM((1, ns, LANES, lanes), bf16),
             pltpu.VMEM((n, 8 * pad, LANES), f32),
             pltpu.VMEM((n, 8 * pad, LANES), f32),
             pltpu.VMEM((16, 16, width), f32),
             pltpu.VMEM((n * pairs, pad, LANES), f32),
-            sems(n), sems(ns), sems(n), sems(ns), sems(n), sems(n), sems(n), sems(ns),
+            sems(n), sems(ns), sems(n), sems(ns), sems(n), sems(n, groups // 8), sems(n), sems(ns),
         ),
         compiler_params=pltpu.CompilerParams(collective_id=0, has_side_effects=True, vmem_limit_bytes=VMEM_LIMIT),
         cost_estimate=pl.CostEstimate(flops=4 * modes * rows * rows * nodes, bytes_accessed=8 << 20, transcendentals=0),
     )(
         field, stiffness, kl_coef, triple_mode, triple_row, triple_col, triple_value, die_elem, die_side, seg_owner,
-        seg_face, die_mortar, int_mortar, bump_coef, int_elem, int_side, sel, sel.T,
+        seg_face, die_mortar, int_mortar, bump_coef.T, int_elem, int_side, sel, sel.T,
     )
 
 

time: 127 us -> 122 us (0.961)
  Pallas kernels: 122 us -> 119 us
  local copies, waits for them, and re-layouts: 4.06 us -> 2.65 us
    pallas_call x1, Pallas kernels: 122 us -> 119 us  [local(): pl.pallas_call(functools.partial(whole_kernel, n=n, ns=ns, cap=cap, faces...]
    unnamed x2 -> x1, local copies, waits for them, and re-layouts: 4.06 us -> 2.65 us
where the time goes in v4:
time: 122 us
  Pallas kernels  119 us (98%)
  local copies, waits for them, and re-layouts  2.65 us (2%)
    pallas_call x1, Pallas kernels, local(): pl.pallas_call(functools.partial(whole_kernel, n=n, ns=ns, cap=cap, faces...  119 us
    unnamed x1, local copies, waits for them, and re-layouts  2.65 us

profile of v4, /device:TPU:11, one launch (start us, length us, event | category | flops | bytes accessed | tf_op | source)
XLA Modules:
  0.0 121.8 jit_solution(16137151408720483747)
XLA Ops:
  0.0 119.1 %shard_map.163 = bf16[42,16384]{1,0:T(8,128)(2,1)} custom-call(bf16[42,16384]{1,0:T(8,128)(2,1)} %field_ref.1, bf16[64,4096]{1,0:T(8,128)(2,1)} %stiff_ref.1, f32[9,64]{1,0:T(8,128)} %kl_ref.1, s32[2688]{0:T(1024)} %mode_ref.1, s32[2688]{0:T(1024)} %row_ref.1, s32[2688]{0:T(1024)} %col_ref.1, f32[2688]{0:T(1024)} %value_ref.1, s32[128]{0:T(128)} %die_elem_ref.1, ...), custom_call_target="tpu_custom_call" | custom-call | flops 4831838208 | bytes 8388608 | tf_op jit(solution)/shard_map/pallas_call | solution.py:598
  119.1 2.7 %copy.19 = bf16[42,16384]{1,0:T(8,128)(2,1)} copy(bf16[42,16384]{1,0:T(8,128)(2,1)} %shard_map.163) | data formatting | bytes 2752512

commit v5 on v4

--- a/solution.py
+++ b/solution.py
@@ -521,15 +521,15 @@
                 hot(iota((elem_rows, faces), 0) == code), table_ref[at_rows(i * faces, faces), :half_lanes])
 
             def delta_step(b, carry):
-                for w in range(4):
-                    blk = 4 * b + w
-                    added = nodal(blk, turn.at[w], size)
+                for w in range(8):
+                    blk = 8 * b + w
+                    added = nodal(blk, turn.at[w] if w < 4 else int_turn.at[w - 4], size)
                     for u in range(4):
                         delta_ref[i * pairs + blk * 4 + u, half * size:(half + 1) * size] = (
                             added[u * size:(u + 1) * size])
                 return carry
 
-            lax.fori_loop(0, blocks // 4, delta_step, 0)
+            lax.fori_loop(0, blocks // 8, delta_step, 0)
             return carry
 
         lax.fori_loop(0, n, gather_step, 0)

time: 122 us -> 125 us (1.025)
  Pallas kernels: 119 us -> 122 us
    pallas_call x1, Pallas kernels: 119 us -> 122 us  [local(): pl.pallas_call(functools.partial(whole_kernel, n=n, ns=ns, cap=cap, faces...]
where the time goes in v5:
time: 125 us; the launch traced here: 124 us
  Pallas kernels  122 us (98%)
  local copies, waits for them, and re-layouts  2.65 us (2%)
    pallas_call x1, Pallas kernels, local(): pl.pallas_call(functools.partial(whole_kernel, n=n, ns=ns, cap=cap, faces...  122 us
    unnamed x1, local copies, waits for them, and re-layouts  2.65 us

profile of v5, /device:TPU:11, one launch (start us, length us, event | category | flops | bytes accessed | tf_op | source)
XLA Modules:
  0.0 124.3 jit_solution(6423259913003789534)
XLA Ops:
  0.0 121.6 %shard_map.163 = bf16[42,16384]{1,0:T(8,128)(2,1)} custom-call(bf16[42,16384]{1,0:T(8,128)(2,1)} %field_ref.1, bf16[64,4096]{1,0:T(8,128)(2,1)} %stiff_ref.1, f32[9,64]{1,0:T(8,128)} %kl_ref.1, s32[2688]{0:T(1024)} %mode_ref.1, s32[2688]{0:T(1024)} %row_ref.1, s32[2688]{0:T(1024)} %col_ref.1, f32[2688]{0:T(1024)} %value_ref.1, s32[128]{0:T(128)} %die_elem_ref.1, ...), custom_call_target="tpu_custom_call" | custom-call | flops 4831838208 | bytes 8388608 | tf_op jit(solution)/shard_map/pallas_call | solution.py:598
  121.6 2.7 %copy.19 = bf16[42,16384]{1,0:T(8,128)(2,1)} copy(bf16[42,16384]{1,0:T(8,128)(2,1)} %shard_map.163) | data formatting | bytes 2752512
